TPU v7x, 32 devices: a whole 2x2x4 slice. The times are simulated.
32 devices in a mesh: ctx: 8 (over y, x, core), head: 4 (over z).
Axes of the slice: x: 2, y: 2, z: 4, core: 2. Of those that a mesh axis runs over, the one named last changes fastest.
Arguments:
- query_vecs: bfloat16 [2048, 4096], P('ctx', 'head'), may hold values from -16 to 16
- key_vecs: bfloat16 [2048, 4096], P('ctx', 'head'), may hold values from -16 to 16
- value_vecs: bfloat16 [2048, 4096], P('ctx', 'head'), may hold values from -9 to 9
- out_grad: bfloat16 [2048, 4096], P('ctx', 'head'), may hold values from -9 to 9
- block_mask: int32 [32, 4], P('ctx'), may hold values from -1 to 31, as said below
- norm_gain: float32 [32, 128], P('head'), may hold values from 0.25 to 1.75
Outputs:
- normed: bfloat16 [2048, 4096], P('ctx', 'head')
- query_grad: bfloat16 [2048, 4096], P('ctx', 'head')
- key_grad: bfloat16 [2048, 4096], P('ctx', 'head')
- value_grad: bfloat16 [2048, 4096], P('ctx', 'head')
- gain_grad: float32 [32, 128], P('head')
Inputs may be any that keep to these rules, and one draw needn't show every extreme that they name: `block_mask`: entry 0 of row b is b; every other entry is -1 (no block) or a block index within 2 of b, and the indices of one row are distinct.
All inputs are finite; a program needn't handle non-finite values.
Results may differ from a plain program's by a relative error of at most 0.0073.
Values may be sent and summed in bfloat16 or wider, within the bound.
A program may use at most 128 MiB of HBM per device.

v0:
```python
import math

import jax
import jax.numpy as jnp
from jax import lax
from jax.sharding import PartitionSpec as P

HEAD_FEATURES = 128
BLOCK = 64
BAND = 2
BLOCKS_DEV = 4
WIDTH = 4096


def shifted(shard, axis, by):
    devices = lax.axis_size(axis)
    pairs = [(i, i + by) for i in range(devices) if 0 <= i + by < devices]
    return lax.ppermute(shard, axis, pairs)


def padded(cells, sides, width):
    for axis, dim in sides:
        count = lax.axis_size(axis)
        ends = count - 1
        head = lax.slice_in_dim(cells, 0, width, axis=dim)
        tail = lax.slice_in_dim(cells, cells.shape[dim] - width, cells.shape[dim], axis=dim)
        cells = jnp.concatenate(
            [
                lax.ppermute(tail, axis, [(i, (i + 1) % count) for i in range(ends)]),
                cells,
                lax.ppermute(head, axis, [((i + 1) % count, i) for i in range(ends)]),
            ],
            axis=dim,
        )
    return cells


def listing(block_list, offset):
    is_live = block_list >= 0
    slot_index = jnp.where(is_live, block_list - offset, 0)
    return (slot_index, is_live)


def pick_rows(extended, slot_index, heads_here):
    picked = extended[slot_index]
    return picked.reshape(
        slot_index.shape[0], slot_index.shape[1] * BLOCK, heads_here, HEAD_FEATURES
    )


def attend_forward(query_block_list, key_row_vectors, value_row_vectors, is_live):
    factor = HEAD_FEATURES ** (-0.5)
    logit_scores = (
        jnp.einsum(
            "bqhd,bkhd->bhqk", query_block_list, key_row_vectors, preferred_element_type=jnp.float32
        )
        * factor
    )
    columns = jnp.repeat(is_live, BLOCK, axis=1)
    logit_scores = jnp.where(columns[:, None, None, :], logit_scores, -1e30)
    highest = jnp.max(logit_scores, axis=-1, keepdims=True)
    powers = jnp.exp(logit_scores - highest)
    total = jnp.sum(powers, axis=-1, keepdims=True)
    weights = powers / total
    rounded_values = weights.astype(jnp.bfloat16)
    attended = jnp.einsum(
        "bhqk,bkhd->bqhd", rounded_values, value_row_vectors, preferred_element_type=jnp.float32
    )
    log_total = (highest + jnp.log(total))[..., 0]
    return (weights, rounded_values, attended, log_total)


def attend_backward(query_block_list, gradient_block_list, ext_blocks, strand):
    (
        slot_index,
        is_live,
        key_row_vectors,
        value_row_vectors,
        weights,
        rounded_values,
        attended,
        log_total,
    ) = strand
    factor = HEAD_FEATURES ** (-0.5)
    weight_gradient = jnp.einsum(
        "bqhd,bkhd->bhqk",
        gradient_block_list,
        value_row_vectors,
        preferred_element_type=jnp.float32,
    )
    centre = jnp.sum(weights * weight_gradient, axis=-1, keepdims=True)
    score_gradient = (weights * (weight_gradient - centre)).astype(jnp.bfloat16)
    query_contributions = (
        jnp.einsum(
            "bhqk,bkhd->bqhd", score_gradient, key_row_vectors, preferred_element_type=jnp.float32
        )
        * factor
    )
    value_contributions = jnp.einsum(
        "bhqk,bqhd->bkhd", rounded_values, gradient_block_list, preferred_element_type=jnp.float32
    )
    key_contributions = (
        jnp.einsum(
            "bhqk,bqhd->bkhd", score_gradient, query_block_list, preferred_element_type=jnp.float32
        )
        * factor
    )
    slots_total = slot_index.shape[0] * slot_index.shape[1]
    placement = (
        jnp.arange(ext_blocks)[:, None] == slot_index.reshape(slots_total)[None, :]
    ) & is_live.reshape(slots_total)[None, :]
    placement = placement.astype(jnp.float32)
    stacked = jnp.stack([key_contributions, value_contributions]).reshape(2, slots_total, -1)
    spread = jnp.einsum("ns,asr->anr", placement, stacked, precision=lax.Precision.HIGHEST)
    features = query_block_list.shape[2] * HEAD_FEATURES
    return (query_contributions, spread.reshape(2, ext_blocks * BLOCK, features), centre[..., 0])


def settle_sum(spread, rim_rows, own_rows):
    lower_rim = spread[:, :rim_rows]
    upper_rim = spread[:, rim_rows + own_rows :]
    from_above = shifted(lower_rim.astype(jnp.bfloat16), "ctx", -1).astype(lower_rim.dtype)
    from_below = shifted(upper_rim.astype(jnp.bfloat16), "ctx", 1).astype(upper_rim.dtype)
    middle = spread[:, rim_rows : rim_rows + own_rows]
    middle = middle.at[:, :rim_rows].add(from_below)
    return middle.at[:, own_rows - rim_rows :].add(from_above)


def body(query_vecs, key_vecs, value_vecs, out_grad, block_mask, norm_gain):
    own_rows = query_vecs.shape[0]
    features = query_vecs.shape[1]
    heads_here = features // HEAD_FEATURES
    rim_rows = BAND * BLOCK
    ext_blocks = BLOCKS_DEV + 2 * BAND
    devices = lax.axis_size("ctx")
    position = lax.axis_index("ctx")
    all_blocks = BLOCKS_DEV * devices
    banded = padded(jnp.stack([key_vecs, value_vecs]), (("ctx", 1),), rim_rows)
    key_ext = banded[0].reshape(ext_blocks, BLOCK, features)
    value_ext = banded[1].reshape(ext_blocks, BLOCK, features)
    full_mask = lax.all_gather(block_mask, "ctx", axis=0, tiled=True)
    first_row = all_blocks - (position + 1) * BLOCKS_DEV
    mirror_rows = lax.dynamic_slice_in_dim(full_mask, first_row, BLOCKS_DEV, 0)[::-1]
    reflected = jnp.where(mirror_rows >= 0, all_blocks - 1 - mirror_rows, -1)
    offset = position * BLOCKS_DEV - BAND
    query_block_list = query_vecs.reshape(BLOCKS_DEV, BLOCK, heads_here, HEAD_FEATURES)
    strands = []
    for block_list in (block_mask, reflected):
        slot_index, is_live = listing(block_list, offset)
        key_row_vectors = pick_rows(key_ext, slot_index, heads_here)
        value_row_vectors = pick_rows(value_ext, slot_index, heads_here)
        weights, rounded_values, attended, log_total = attend_forward(
            query_block_list, key_row_vectors, value_row_vectors, is_live
        )
        strands.append(
            (
                slot_index,
                is_live,
                key_row_vectors,
                value_row_vectors,
                weights,
                rounded_values,
                attended,
                log_total,
            )
        )
    mixed_sum = (strands[0][6] + strands[1][6]).reshape(own_rows, features)
    squares = lax.psum(jnp.sum(mixed_sum * mixed_sum, axis=1), "head")
    rms_root = jnp.sqrt(squares / WIDTH + 1e-06)[:, None]
    flat_gain = norm_gain.reshape(features)
    normed = (flat_gain * mixed_sum / rms_root).astype(jnp.bfloat16)
    grad_values = out_grad.astype(jnp.float32)
    scaled_grad = flat_gain * grad_values
    inner_sum = lax.psum(jnp.sum(scaled_grad * mixed_sum, axis=1), "head")[:, None] / WIDTH
    mixed_grad = (
        scaled_grad / rms_root - mixed_sum * inner_sum / (rms_root * rms_root * rms_root)
    ).astype(jnp.bfloat16)
    gain_part = jnp.sum(grad_values * mixed_sum / rms_root, axis=0).reshape(
        heads_here, HEAD_FEATURES
    )
    gain_grad = lax.psum(gain_part, "ctx") / math.sqrt(own_rows * devices)
    gradient_block_list = mixed_grad.reshape(BLOCKS_DEV, BLOCK, heads_here, HEAD_FEATURES)
    query_one, spread_one, centre_one = attend_backward(
        query_block_list, gradient_block_list, ext_blocks, strands[0]
    )
    query_two, spread_two, centre_two = attend_backward(
        query_block_list, gradient_block_list, ext_blocks, strands[1]
    )
    settled = settle_sum(spread_one + spread_two, rim_rows, own_rows)
    query_grad = (query_one + query_two).reshape(own_rows, features).astype(jnp.bfloat16)
    key_grad = settled[0].astype(jnp.bfloat16)
    value_grad = settled[1].astype(jnp.bfloat16)
    return (normed, query_grad, key_grad, value_grad, gain_grad)


def solution(mesh):
    return jax.shard_map(
        body,
        mesh=mesh,
        in_specs=(
            P("ctx", "head"),
            P("ctx", "head"),
            P("ctx", "head"),
            P("ctx", "head"),
            P("ctx", None),
            P("head", None),
        ),
        out_specs=(
            P("ctx", "head"),
            P("ctx", "head"),
            P("ctx", "head"),
            P("ctx", "head"),
            P("head", None),
        ),
        check_vma=False,
    )
```

profile of v0, /device:TPU:4, one launch (start us, length us, event | category | flops | bytes accessed | tf_op | source)
XLA Modules:
  0.0 177.0 jit_solution(70778081247639693)
XLA Ops:
  2.0 2.8 %collective-permute-start.1 = (bf16[2,128,1024]{2,1,0:T(8,128)(2,1)S(1)}, bf16[2,128,1024]{2,1,0:T(8,128)(2,1)}, u32[]{:S(2)}, u32[]{:S(2)}) collective-permute-start(bf16[2,128,1024]{2,1,0:T(8,128)(2,1)S(1)} %get-tuple-element.44), channel_id=1, source_target_pairs={{4,0},{8,4},{12,8},{16,12},{20,16},{24,20},{28,24},{5,1},{9,5},{13... | collective-permute-start | bytes 1572872 | tf_op jit(solution)/shard_map/ppermute | solution.py:31
  4.8 1.9 %collective-permute-start = (bf16[2,128,1024]{2,1,0:T(8,128)(2,1)S(1)}, bf16[2,128,1024]{2,1,0:T(8,128)(2,1)}, u32[]{:S(2)}, u32[]{:S(2)}) collective-permute-start(bf16[2,128,1024]{2,1,0:T(8,128)(2,1)S(1)} %get-tuple-element.43), channel_id=1, source_target_pairs={{0,4},{4,8},{8,12},{12,16},{16,20},{20,24},{24,28},{1,5},{5,9},{9,... | collective-permute-start | bytes 1572872 | tf_op jit(solution)/shard_map/ppermute | solution.py:29
  6.9 14.4 %all-gather = s32[8,4,4]{2,1,0:T(4,128)S(1)} all-gather(s32[1,4,4]{2,1,0:T(4,128)S(1)} %bitcast.150), channel_id=1, replica_groups=mesh['ctx'=8,'head'=4] {'ctx'}, dimensions={0}, use_global_device_ids=true | all-gather | bytes 576 | tf_op jit(solution)/shard_map/all_gather | solution.py:141
  24.6 2.0 %gather_fusion.2 = bf16[16,64,1024]{2,1,0:T(8,128)(2,1)} fusion(bf16[8,64,1024]{2,1,0:T(8,128)(2,1)S(1)} %bitcast.115, s32[1024]{0:T(1024)S(1)} %pad_clamp_fusion), kind=kCustom, calls=%fused_computation.2 | custom fusion | bytes 4194368 | tf_op jit(solution)/shard_map/gather | solution.py:45
  26.7 2.0 %gather_fusion.3 = bf16[16,64,1024]{2,1,0:T(8,128)(2,1)} fusion(bf16[8,64,1024]{2,1,0:T(8,128)(2,1)S(1)} %bitcast.113, s32[1024]{0:T(1024)S(1)} %pad_clamp_fusion), kind=kCustom, calls=%fused_computation.3 | custom fusion | bytes 4194368 | tf_op jit(solution)/shard_map/gather | solution.py:45
  28.6 2.0 %gather_fusion = bf16[16,64,1024]{2,1,0:T(8,128)(2,1)} fusion(bf16[8,64,1024]{2,1,0:T(8,128)(2,1)S(1)} %bitcast.116, s32[1024]{0:T(1024)S(1)} %pad_clamp_fusion.1), kind=kCustom, calls=%fused_computation | custom fusion | bytes 4194368 | tf_op jit(solution)/shard_map/gather | solution.py:45
  30.6 2.0 %gather_fusion.1 = bf16[16,64,1024]{2,1,0:T(8,128)(2,1)} fusion(bf16[8,64,1024]{2,1,0:T(8,128)(2,1)S(1)} %bitcast.114, s32[1024]{0:T(1024)S(1)} %pad_clamp_fusion.1), kind=kCustom, calls=%fused_computation.1 | custom fusion | bytes 4194368 | tf_op jit(solution)/shard_map/gather | solution.py:45
  32.7 2.4 %copy.102 = bf16[128,8,8,128]{3,2,1,0:T(8,128)(2,1)S(1)} copy(bf16[128,8,8,128]{3,1,2,0:T(8,128)(2,1)} %bitcast.127) | data formatting | bytes 4194304
  35.7 2.5 %copy-done.8 = bf16[16,64,1024]{2,1,0:T(8,128)(2,1)S(1)} copy-done((bf16[16,64,1024]{2,1,0:T(8,128)(2,1)S(1)}, bf16[16,64,1024]{2,1,0:T(8,128)(2,1)}, u32[]{:S(2)}) %copy-start.8) | copy-done | bytes 2097176
  47.4 12.1 %psum.21 = f32[256]{0:T(256)S(1)} all-reduce(f32[256]{0:T(256)S(1)} %reduce_sum.68), channel_id=1, replica_groups=mesh['ctx'=8,'head'=4] {'head'}, use_global_device_ids=true, to_apply=%region_5.6 | all-reduce | flops 256 | bytes 2048 | tf_op jit(solution)/shard_map/psum | solution.py:168
  62.7 8.5 %psum.22 = f32[256]{0:T(256)S(1)} all-reduce(f32[256]{0:T(256)S(1)} %get-tuple-element.30), channel_id=1, replica_groups=mesh['ctx'=8,'head'=4] {'head'}, use_global_device_ids=true, to_apply=%region_7.8 | all-reduce | flops 256 | bytes 2048 | tf_op jit(solution)/shard_map/psum | solution.py:174
  71.3 2.6 %fusion.75 = (bf16[32,8,8,128]{3,1,2,0:T(8,128)(2,1)S(1)}, bf16[256,1024]{1,0:T(8,128)(2,1)}) fusion(f32[256]{0:T(256)S(1)} %get-tuple-element.45, f32[256]{0:T(256)S(1)} %broadcast_multiply_fusion.1, f32[32,8,8,128]{3,2,1,0:T(8,128)} %bitcast.126, f32[256]{0:T(256)S(1)} %get-tuple-element.46, bf16[256,1024]{1,0:T(8,128)(2,1)S(1)} %copy-done.19, ...), kind=kLoop, calls=%fused_computation.94 | loop fusion | flops 2621440 | bytes 2628608
  74.0 2.7 %multiply_reduce_fusion = (f32[4,8,64]{2,1,0:T(8,128)S(1)}, f32[4,8,64,256]{3,2,1,0:T(8,128)S(1)}) fusion(f32[4,8,64,256]{3,2,1,0:T(8,128)} %copy-done.17, f32[4,8,64]{2,1,0:T(8,128)S(1)} %get-tuple-element.47, bf16[4,256,8,128]{3,2,1,0:T(8,128)(2,1)S(1)} %bitcast.132, bf16[4,64,8,128]{3,2,1,0:T(8,128)(2,1)S(1)} %bitcast.142), kind=kOutput, calls=%fused_computation.29 | convolution fusion | flops 135788544 | bytes 6832128 | tf_op jit(solution)/shard_map/bqhd,bkhd->bhqk/dot_general | solution.py:85
  76.8 2.2 %multiply_reduce_fusion.1 = (f32[4,8,64]{2,1,0:T(8,128)S(1)}, f32[4,8,64,256]{3,2,1,0:T(8,128)}) fusion(f32[4,8,64,256]{3,2,1,0:T(8,128)S(1)} %copy-done.12, f32[4,8,64]{2,1,0:T(8,128)S(1)} %get-tuple-element.49, bf16[4,256,8,128]{3,2,1,0:T(8,128)(2,1)S(1)} %bitcast.134, bf16[4,64,8,128]{3,2,1,0:T(8,128)(2,1)S(1)} %bitcast.143), kind=kOutput, calls=%fused_computation.31 | convolution fusion | flops 135788544 | bytes 6832128 | tf_op jit(solution)/shard_map/bqhd,bkhd->bhqk/dot_general | solution.py:85
  79.0 2.9 %convolution_bitcast_fusion.1 = f32[4,256,8,128]{1,3,2,0:T(8,128)} fusion(bf16[4,64,8,128]{3,2,1,0:T(8,128)(2,1)S(1)} %bitcast.144, f32[4,8,64,256]{3,2,1,0:T(8,128)S(1)} %copy-done.12, f32[4,8,64]{2,1,0:T(8,128)S(1)} %get-tuple-element.49), kind=kOutput, calls=%fused_computation.18 | convolution fusion | flops 135266304 | bytes 6823936 | tf_op jit(solution)/shard_map/bhqk,bqhd->bkhd/dot_general | solution.py:99
  81.9 2.9 %convolution_bitcast_fusion = f32[4,256,8,128]{1,3,2,0:T(8,128)} fusion(bf16[4,64,8,128]{3,2,1,0:T(8,128)(2,1)S(1)} %bitcast.145, f32[4,8,64,256]{3,2,1,0:T(8,128)S(1)} %copy-done.18, f32[4,8,64]{2,1,0:T(8,128)S(1)} %get-tuple-element.47), kind=kOutput, calls=%fused_computation.17 | convolution fusion | flops 135266304 | bytes 6823936 | tf_op jit(solution)/shard_map/bhqk,bqhd->bkhd/dot_general | solution.py:99
  87.8 2.7 %multiply_bitcast_fusion = f32[4,256,8,128]{3,1,2,0:T(8,128)} fusion(bf16[4,8,64,256]{3,2,1,0:T(8,128)(2,1)S(1)} %multiply_convert_fusion, bf16[4,64,8,128]{3,2,1,0:T(8,128)(2,1)S(1)} %bitcast.123), kind=kOutput, calls=%fused_computation.15 | convolution fusion | flops 135266304 | bytes 5767168 | tf_op jit(solution)/shard_map/bhqk,bqhd->bkhd/dot_general | solution.py:103
  90.5 5.3 %copy.87 = f32[4,256,8,128]{3,2,1,0:T(8,128)} copy(f32[4,256,8,128]{1,3,2,0:T(8,128)} %convolution_bitcast_fusion.1) | data formatting | bytes 8388608 | tf_op jit(solution)/shard_map/bhqk,bqhd->bkhd/transpose | solution.py:99
  95.8 3.9 %stack.31 = f32[1,16,65536]{2,1,0:T(8,128)} reshape(f32[4,256,8,128]{3,2,1,0:T(8,128)} %copy.87) | data formatting | bytes 8388608 | tf_op jit(solution)/shard_map/stack | solution.py:113
  99.7 2.5 %multiply_convert_fusion.1 = bf16[4,8,64,256]{3,2,1,0:T(8,128)(2,1)S(1)} fusion(f32[4,8,64,256]{3,2,1,0:T(8,128)} %get-tuple-element.56, f32[4,8,64]{2,1,0:T(8,128)S(1)} %get-tuple-element.55, f32[4,8,64,256]{3,2,1,0:T(8,128)} %copy-done.11, f32[4,8,64]{2,1,0:T(8,128)S(1)} %get-tuple-element.49), kind=kLoop, calls=%fused_computation.30 | loop fusion | flops 2097152 | bytes 5259264 | tf_op jit(solution)/shard_map/convert_element_type | solution.py:92
  104.0 4.4 %copy.85 = f32[4,256,8,128]{3,2,1,0:T(8,128)} copy(f32[4,256,8,128]{3,1,2,0:T(8,128)S(1)} %multiply_bitcast_fusion.1) | data formatting | bytes 8388608 | tf_op jit(solution)/shard_map/mul | solution.py:103
  108.4 3.9 %stack.30 = f32[1,16,65536]{2,1,0:T(8,128)} reshape(f32[4,256,8,128]{3,2,1,0:T(8,128)} %copy.85) | data formatting | bytes 8388608 | tf_op jit(solution)/shard_map/stack | solution.py:113
  112.3 5.3 %copy.93 = f32[4,256,8,128]{3,2,1,0:T(8,128)} copy(f32[4,256,8,128]{1,3,2,0:T(8,128)} %convolution_bitcast_fusion) | data formatting | bytes 8388608 | tf_op jit(solution)/shard_map/bhqk,bqhd->bkhd/transpose | solution.py:99
  117.6 3.9 %stack.34 = f32[1,16,65536]{2,1,0:T(8,128)} reshape(f32[4,256,8,128]{3,2,1,0:T(8,128)} %copy.93) | data formatting | bytes 8388608 | tf_op jit(solution)/shard_map/stack | solution.py:113
  121.5 6.6 %copy.91 = f32[4,256,8,128]{3,2,1,0:T(8,128)} copy(f32[4,256,8,128]{3,1,2,0:T(8,128)} %multiply_bitcast_fusion) | data formatting | bytes 8388608 | tf_op jit(solution)/shard_map/mul | solution.py:103
  128.1 3.9 %stack.33 = f32[1,16,65536]{2,1,0:T(8,128)} reshape(f32[4,256,8,128]{3,2,1,0:T(8,128)} %copy.91) | data formatting | bytes 8388608 | tf_op jit(solution)/shard_map/stack | solution.py:113
  132.0 5.6 %fusion.3 = f32[2,65536,8]{1,2,0:T(8,128)S(1)} fusion(f32[1,16,65536]{2,1,0:T(8,128)} %stack.31, f32[1,16,65536]{2,1,0:T(8,128)} %stack.30, s32[16]{0:T(128)S(1)} %eq.31, pred[16]{0:T(512)(128)(4,1)S(1)} %and.27), kind=kOutput, calls=%fused_computation.8 | convolution fusion | flops 203424000 | bytes 12582992 | tf_op jit(solution)/shard_map/ns,asr->anr/dot_general | solution.py:114
  137.9 4.7 %fusion.2 = f32[2,8,65536]{2,1,0:T(8,128)} fusion(f32[2,65536,8]{1,2,0:T(8,128)S(1)} %fusion.3, f32[1,16,65536]{2,1,0:T(8,128)S(1)} %copy-done.2, f32[1,16,65536]{2,1,0:T(8,128)S(1)} %copy-done.3, s32[16]{0:T(128)S(1)} %eq.35, pred[16]{0:T(512)(128)(4,1)S(1)} %and.30), kind=kOutput, calls=%fused_computation.7 | convolution fusion | flops 204472576 | bytes 16777296 | tf_op jit(solution)/shard_map/ns,asr->anr/dot_general | solution.py:114
  142.7 3.9 %add.72 = f32[2,512,1024]{2,1,0:T(8,128)} reshape(f32[2,8,65536]{2,1,0:T(8,128)} %fusion.2) | data formatting | bytes 8388608 | tf_op jit(solution)/shard_map/add | solution.py:189
  146.6 2.5 %convert.8 = bf16[2,512,1024]{2,1,0:T(8,128)(2,1)S(1)} convert(f32[2,512,1024]{2,1,0:T(8,128)} %add.72) | non-fusion elementwise | flops 1048576 | bytes 6291456 | tf_op jit(solution)/shard_map/convert.3
  152.1 4.5 %collective-permute-start.3 = (bf16[2,128,1024]{2,1,0:T(8,128)(2,1)}, bf16[2,128,1024]{2,1,0:T(8,128)(2,1)S(1)}, u32[]{:S(2)}, u32[]{:S(2)}) collective-permute-start(bf16[2,128,1024]{2,1,0:T(8,128)(2,1)} %get-tuple-element.35), channel_id=1, source_target_pairs={{4,0},{8,4},{12,8},{16,12},{20,16},{24,20},{28,24},{5,1},{9,5},{13... | collective-permute-start | bytes 1572872 | tf_op jit(solution)/shard_map/ppermute | solution.py:18
  158.4 15.2 %psum.23 = f32[8,128]{1,0:T(8,128)S(1)} all-reduce(f32[8,128]{1,0:T(8,128)S(1)} %bitcast.149), channel_id=1, replica_groups=mesh['ctx'=8,'head'=4] {'ctx'}, use_global_device_ids=true, to_apply=%region_11.12 | all-reduce | flops 1024 | bytes 8192 | tf_op jit(solution)/shard_map/psum | solution.py:181
  (113 shorter events, 31.2 us)
Async XLA Ops:
  0.6 22.4 %copy-start.20 = (bf16[256,1024]{1,0:T(8,128)(2,1)S(1)}, bf16[256,1024]{1,0:T(8,128)(2,1)}, u32[]{:S(2)}) copy-start(bf16[256,1024]{1,0:T(8,128)(2,1)} %param.11) | copy-start | bytes 1572868
  0.6 22.4 %copy-start.21 = (bf16[256,1024]{1,0:T(8,128)(2,1)S(1)}, bf16[256,1024]{1,0:T(8,128)(2,1)}, u32[]{:S(2)}) copy-start(bf16[256,1024]{1,0:T(8,128)(2,1)} %param.12) | copy-start | bytes 1572868
  0.7 6.1 %copy-start.24 = (s32[4,4]{1,0:T(4,128)S(1)}, s32[4,4]{1,0:T(4,128)}, u32[]{:S(2)}) copy-start(s32[4,4]{1,0:T(4,128)} %param.14) | copy-start | bytes 196
  0.7 21.0 %copy-start.22 = (bf16[256,1024]{1,0:T(8,128)(2,1)S(1)}, bf16[256,1024]{1,0:T(8,128)(2,1)}, u32[]{:S(2)}) copy-start(bf16[256,1024]{1,0:T(8,128)(2,1)} %param.10) | copy-start | bytes 1572868
  2.0 21.0 %collective-permute-start.1 = (bf16[2,128,1024]{2,1,0:T(8,128)(2,1)S(1)}, bf16[2,128,1024]{2,1,0:T(8,128)(2,1)}, u32[]{:S(2)}, u32[]{:S(2)}) collective-permute-start(bf16[2,128,1024]{2,1,0:T(8,128)(2,1)S(1)} %get-tuple-element.44), channel_id=1, source_target_pairs={{4,0},{8,4},{12,8},{16,12},{20,16},{24,20},{28,24},{5,1},{9,5},{13... | collective-permute-start | bytes 1572872 | tf_op jit(solution)/shard_map/ppermute | solution.py:31
  4.8 18.2 %collective-permute-start = (bf16[2,128,1024]{2,1,0:T(8,128)(2,1)S(1)}, bf16[2,128,1024]{2,1,0:T(8,128)(2,1)}, u32[]{:S(2)}, u32[]{:S(2)}) collective-permute-start(bf16[2,128,1024]{2,1,0:T(8,128)(2,1)S(1)} %get-tuple-element.43), channel_id=1, source_target_pairs={{0,4},{4,8},{8,12},{12,16},{16,20},{20,24},{24,28},{1,5},{5,9},{9,... | collective-permute-start | bytes 1572872 | tf_op jit(solution)/shard_map/ppermute | solution.py:29
  32.7 2.4 %copy-start.7 = (bf16[16,64,1024]{2,1,0:T(8,128)(2,1)S(1)}, bf16[16,64,1024]{2,1,0:T(8,128)(2,1)}, u32[]{:S(2)}) copy-start(bf16[16,64,1024]{2,1,0:T(8,128)(2,1)} %gather_fusion.3) | copy-start | bytes 6291460
  35.0 9.2 %copy-start.13 = (bf16[128,8,8,128]{3,2,1,0:T(8,128)(2,1)}, bf16[128,8,8,128]{3,2,1,0:T(8,128)(2,1)S(1)}, u32[]{:S(2)}) copy-start(bf16[128,8,8,128]{3,2,1,0:T(8,128)(2,1)S(1)} %copy.102) | copy-start | bytes 6291460
  35.1 3.1 %copy-start.8 = (bf16[16,64,1024]{2,1,0:T(8,128)(2,1)S(1)}, bf16[16,64,1024]{2,1,0:T(8,128)(2,1)}, u32[]{:S(2)}) copy-start(bf16[16,64,1024]{2,1,0:T(8,128)(2,1)} %gather_fusion) | copy-start | bytes 6291460
  35.7 4.7 %copy-start = (bf16[128,8,8,128]{3,2,1,0:T(8,128)(2,1)}, bf16[128,8,8,128]{3,2,1,0:T(8,128)(2,1)S(1)}, u32[]{:S(2)}) copy-start(bf16[128,8,8,128]{3,2,1,0:T(8,128)(2,1)S(1)} %copy.101) | copy-start | bytes 6291460
  38.2 1.6 copy-start.9
  38.8 6.5 %copy-start.15 = (bf16[128,8,8,128]{3,2,1,0:T(8,128)(2,1)}, bf16[128,8,8,128]{3,2,1,0:T(8,128)(2,1)S(1)}, u32[]{:S(2)}) copy-start(bf16[128,8,8,128]{3,2,1,0:T(8,128)(2,1)S(1)} %copy.100) | copy-start | bytes 6291460
  43.2 1.4 copy-start.17
  44.2 1.3 copy-start.11
  47.3 15.1 %copy-start.19 = (bf16[256,1024]{1,0:T(8,128)(2,1)S(1)}, bf16[256,1024]{1,0:T(8,128)(2,1)}, u32[]{:S(2)}) copy-start(bf16[256,1024]{1,0:T(8,128)(2,1)} %param.13) | copy-start | bytes 1572868
  47.3 15.1 %copy-start.23 = (f32[8,128]{1,0:T(8,128)S(1)}, f32[8,128]{1,0:T(8,128)}, u32[]{:S(2)}) copy-start(f32[8,128]{1,0:T(8,128)} %param.15) | copy-start | bytes 12292
  61.3 1.1 copy-start.4
  71.3 2.7 %copy-start.14 = (bf16[128,8,8,128]{3,2,1,0:T(8,128)(2,1)S(1)}, bf16[128,8,8,128]{3,2,1,0:T(8,128)(2,1)}, u32[]{:S(2)}) copy-start(bf16[128,8,8,128]{3,2,1,0:T(8,128)(2,1)} %copy-done.13) | copy-start | bytes 6291460
  74.0 2.7 %copy-start.12 = (f32[4,8,64,256]{3,2,1,0:T(8,128)S(1)}, f32[4,8,64,256]{3,2,1,0:T(8,128)}, u32[]{:S(2)}) copy-start(f32[4,8,64,256]{3,2,1,0:T(8,128)} %copy-done.11) | copy-start | bytes 6291460
  74.0 2.8 %copy-start.16 = (bf16[128,8,8,128]{3,2,1,0:T(8,128)(2,1)S(1)}, bf16[128,8,8,128]{3,2,1,0:T(8,128)(2,1)}, u32[]{:S(2)}) copy-start(bf16[128,8,8,128]{3,2,1,0:T(8,128)(2,1)} %copy-done.15) | copy-start | bytes 6291460
  79.0 2.9 %copy-start.18 = (f32[4,8,64,256]{3,2,1,0:T(8,128)S(1)}, f32[4,8,64,256]{3,2,1,0:T(8,128)}, u32[]{:S(2)}) copy-start(f32[4,8,64,256]{3,2,1,0:T(8,128)} %copy-done.17) | copy-start | bytes 6291460
  84.8 1.6 copy-start.1
  102.3 1.0 copy-start.5
  132.0 5.6 %copy-start.2 = (f32[1,16,65536]{2,1,0:T(8,128)S(1)}, f32[1,16,65536]{2,1,0:T(8,128)}, u32[]{:S(2)}) copy-start(f32[1,16,65536]{2,1,0:T(8,128)} %stack.34) | copy-start | bytes 12582916
  132.0 5.9 %copy-start.3 = (f32[1,16,65536]{2,1,0:T(8,128)S(1)}, f32[1,16,65536]{2,1,0:T(8,128)}, u32[]{:S(2)}) copy-start(f32[1,16,65536]{2,1,0:T(8,128)} %stack.33) | copy-start | bytes 12582916
  149.1 7.5 %copy-start.6 = (bf16[4,8,64,256]{3,2,1,0:T(8,128)(2,1)S(1)}, bf16[4,8,64,256]{3,2,1,0:T(8,128)(2,1)}, u32[]{:S(2)}) copy-start(bf16[4,8,64,256]{3,2,1,0:T(8,128)(2,1)} %copy-done.5) | copy-start | bytes 3145732
  149.1 7.5 %copy-start.10 = (f32[4,8,128,64]{2,3,1,0:T(8,128)S(1)}, f32[4,8,128,64]{2,3,1,0:T(8,128)}, u32[]{:S(2)}) copy-start(f32[4,8,128,64]{2,3,1,0:T(8,128)} %fusion.22) | copy-start | bytes 3145732
  150.2 24.0 %collective-permute-start.2 = (bf16[2,128,1024]{2,1,0:T(8,128)(2,1)}, bf16[2,128,1024]{2,1,0:T(8,128)(2,1)S(1)}, u32[]{:S(2)}, u32[]{:S(2)}) collective-permute-start(bf16[2,128,1024]{2,1,0:T(8,128)(2,1)} %get-tuple-element.36), channel_id=1, source_target_pairs={{0,4},{4,8},{8,12},{12,16},{16,20},{20,24},{24,28},{1,5},{5,9},{9,... | collective-permute-start | bytes 1572872 | tf_op jit(solution)/shard_map/ppermute | solution.py:18
  152.1 23.5 %collective-permute-start.3 = (bf16[2,128,1024]{2,1,0:T(8,128)(2,1)}, bf16[2,128,1024]{2,1,0:T(8,128)(2,1)S(1)}, u32[]{:S(2)}, u32[]{:S(2)}) collective-permute-start(bf16[2,128,1024]{2,1,0:T(8,128)(2,1)} %get-tuple-element.35), channel_id=1, source_target_pairs={{4,0},{8,4},{12,8},{16,12},{20,16},{24,20},{28,24},{5,1},{9,5},{13... | collective-permute-start | bytes 1572872 | tf_op jit(solution)/shard_map/ppermute | solution.py:18
  157.1 17.0 %slice-start = ((f32[2,512,1024]{2,1,0:T(8,128)}), f32[2,256,1024]{2,1,0:T(8,128)S(1)}, s32[]{:S(2)}) async-start(f32[2,512,1024]{2,1,0:T(8,128)} %add.72), calls=%async_computation | async-start | bytes 4194304 | tf_op jit(solution)/shard_map/slice | solution.py:124
where the time goes:
time: 179 us; the launch traced here: 177 us
  local copies, waits for them, and re-layouts  67.9 us (38%)
  blocking collectives  50.2 us (28%)
  matrix products  30.6 us (17%)
  other arithmetic  16 us (9%)
  starting transfers between devices  11.2 us (6%)
    another operation x4, local copies, waits for them, and re-layouts, attend_backward(): jnp.stack([key_contributions, value_contributions])  15.7 us
    psum x1, blocking collectives, body(): gain_grad = lax.psum(gain_part, 'ctx') / math.sqrt(own_rows * devices)  15.2 us
    all_gather x1, blocking collectives, body(): full_mask = lax.all_gather(block_mask, 'ctx', axis=0, tiled=True)  14.4 us
    unnamed x59, local copies, waits for them, and re-layouts  12.8 us
    psum x1, blocking collectives, body(): squares = lax.psum(jnp.sum(mixed_sum * mixed_sum, axis=1), 'head')  12.1 us
    mul x2, local copies, waits for them, and re-layouts, attend_backward(): jnp.einsum('bhqk,bqhd->bkhd', score_gradient, query_block_list, preferred...  10.9 us
    transpose x2, local copies, waits for them, and re-layouts, attend_backward(): jnp.einsum('bhqk,bqhd->bkhd', rounded_values, gradient_block_list, prefer...  10.5 us
    dot_general x2, matrix products, attend_backward(): jnp.einsum('ns,asr->anr', placement, stacked, precision=lax.Precision.HIG...  10.4 us
  transfers between devices with their start and end apart: 4, of which 0 were waited for; matrix products, arithmetic and copies ran while one was open for 3% of the time, Pallas kernels for 0%

commit v1 on v0

v1 whole, which is shorter than its diff:
```python
import functools
import math

import jax
import jax.numpy as jnp
from jax import lax
from jax.experimental import pallas as pl
from jax.experimental.pallas import tpu as pltpu
from jax.sharding import PartitionSpec as P

D = 128
BLOCK = 64
BAND = 2
RIM = BAND * BLOCK
PAIR = 2 * BLOCK
WINDOW = PAIR + 2 * RIM
MESH = pl.DeviceIdType.MESH
NT = (((1,), (1,)), ((), ()))
TN = (((0,), (0,)), ((), ()))
NN = (((1,), (0,)), ((), ()))


def dot(a, b, dims):
    return lax.dot_general(a, b, dims, preferred_element_type=jnp.float32)


def kernel(
    n_ctx, n_head,
    q_hbm, k_hbm, v_hbm, og_hbm, mask_ref, gain_ref,
    normed_hbm, dq_hbm, dk_hbm, dv_hbm, gg_ref,
    q, kext, vext, og, mine, theirs, bias, w1s, w2s, mixed, sq, inner, sall, invs, coefs,
    grad, gall, normed, dq, dk, dv, dko, dvo, out_halo, in_halo,
    load_sem, fsend, frecv, msend, mrecv, ssend, srecv, gsend, grecv, bsend, brecv, store_sem,
):
    pos = lax.axis_index("ctx")
    me_h = lax.axis_index("head")
    rows, features = q.shape
    heads = features // D
    pairs = rows // PAIR
    blocks_dev = rows // BLOCK
    width = features * n_head
    scale = D ** -0.5
    last = n_ctx - 1

    loads = [
        pltpu.make_async_copy(k_hbm, kext.at[pl.ds(RIM, rows)], load_sem.at[0]),
        pltpu.make_async_copy(q_hbm, q, load_sem.at[1]),
        pltpu.make_async_copy(v_hbm, vext.at[pl.ds(RIM, rows)], load_sem.at[2]),
        pltpu.make_async_copy(og_hbm, og, load_sem.at[3]),
    ]
    for copy in loads:
        copy.start()

    barrier = pltpu.get_barrier_semaphore()
    for o in range(1, n_ctx):
        pl.semaphore_signal(barrier, inc=1, device_id=(lax.rem(pos + o, n_ctx), me_h), device_id_type=MESH)
    for o in range(1, n_head):
        pl.semaphore_signal(barrier, inc=1, device_id=(pos, lax.rem(me_h + o, n_head)), device_id_type=MESH)
    mine[...] = jnp.zeros_like(mine)
    mine[0:blocks_dev, 0:mask_ref.shape[1]] = mask_ref[...]
    sall[me_h] = jnp.zeros(sall.shape[1:], jnp.float32)
    sq[...] = jnp.zeros_like(sq)
    inner[...] = jnp.zeros_like(inner)

    @pl.when(pos == 0)
    def _():
        kext[0:RIM, :] = jnp.zeros((RIM, features), kext.dtype)
        vext[0:RIM, :] = jnp.zeros((RIM, features), vext.dtype)

    @pl.when(pos == last)
    def _():
        kext[rows + RIM :, :] = jnp.zeros((RIM, features), kext.dtype)
        vext[rows + RIM :, :] = jnp.zeros((RIM, features), vext.dtype)

    pl.semaphore_wait(barrier, n_ctx - 1 + n_head - 1)

    def cols(h):
        return pl.ds(pl.multiple_of(h * D, D), D)

    right = jnp.minimum(pos + 1, last)
    left = jnp.maximum(pos - 1, 0)

    def halo(way, kv, h):
        src = (k_hbm, v_hbm)[kv]
        dst = (kext, vext)[kv]
        from_row, to_row = ((rows - RIM, 0), (0, rows + RIM))[way]
        return pltpu.make_async_remote_copy(
            src_ref=src.at[pl.ds(from_row, RIM), cols(h)],
            dst_ref=dst.at[pl.ds(to_row, RIM), cols(h)],
            send_sem=fsend.at[way, kv, h],
            recv_sem=frecv.at[way, kv, h],
            device_id=((right, left)[way], me_h),
            device_id_type=MESH,
        )

    mirror = pltpu.make_async_remote_copy(
        src_ref=mine, dst_ref=theirs, send_sem=msend, recv_sem=mrecv,
        device_id=(last - pos, me_h), device_id_type=MESH,
    )
    mirror.start()

    def send_halos(h, carry):
        for kv in range(2):
            @pl.when(pos < last)
            def _():
                halo(0, kv, h).start()

            @pl.when(pos > 0)
            def _():
                halo(1, kv, h).start()
        return carry

    lax.fori_loop(0, heads, send_halos, 0)
    mirror.wait_recv()

    all_blocks = blocks_dev * n_ctx
    row_block = lax.broadcasted_iota(jnp.int32, (WINDOW, PAIR), 0) // BLOCK
    second = lax.broadcasted_iota(jnp.int32, (8, PAIR), 1) >= BLOCK
    for strand in range(2):
        table = (mine, theirs)[strand]
        for p in range(pairs):
            first = pos * blocks_dev - BAND + 2 * p
            live = None
            for n in range(mask_ref.shape[1]):
                lists = []
                for b in (2 * p, 2 * p + 1):
                    r = b if strand == 0 else blocks_dev - 1 - b
                    lists.append(jnp.broadcast_to(table[r : r + 1, n : n + 1], (8, PAIR)))
                entry = jnp.where(second, lists[1], lists[0])
                if strand == 1:
                    target = all_blocks - 1 - entry
                else:
                    target = entry
                target = jnp.where(entry >= 0, target - first, -1)[0:1]
                hit = row_block == target
                live = hit if live is None else live | hit
            bias[strand, p] = jnp.where(live, 0.0, -1e30)

    for copy in loads:
        copy.wait()

    def forward(h, carry):
        c = cols(h)
        for kv in range(2):
            @pl.when(pos > 0)
            def _():
                halo(0, kv, h).wait_recv()

            @pl.when(pos < last)
            def _():
                halo(1, kv, h).wait_recv()
        gain = gain_ref[pl.ds(h, 1), :]
        for p in range(pairs):
            r = pl.ds(p * PAIR, PAIR)
            w = pl.ds(p * PAIR, WINDOW)
            scores = dot(kext[w, c], q[r, c], NT) * scale
            total = None
            for strand, kept in ((0, w1s), (1, w2s)):
                s = scores + bias[strand, p]
                e = jnp.exp(s - jnp.max(s, axis=0, keepdims=True))
                e = e * (1.0 / jnp.sum(e, axis=0, keepdims=True))
                kept[h, p] = e
                total = e if total is None else total + e
            m = dot(total.astype(jnp.bfloat16), vext[w, c], TN)
            mixed[r, c] = m
            sq[r, :] += m * m
            inner[r, :] += gain * og[r, c].astype(jnp.float32) * m
        return carry

    lax.fori_loop(0, heads, forward, 0)

    for p in range(pairs):
        r = slice(p * PAIR, (p + 1) * PAIR)
        sall[me_h, p : p + 1, :] = jnp.sum(sq[r, :].T, axis=0, keepdims=True)
        sall[me_h, pairs + p : pairs + p + 1, :] = jnp.sum(inner[r, :].T, axis=0, keepdims=True)

    def stat(slot, o, to):
        return pltpu.make_async_remote_copy(
            src_ref=sall.at[slot], dst_ref=sall.at[slot],
            send_sem=ssend.at[o], recv_sem=srecv.at[slot],
            device_id=(pos, to), device_id_type=MESH,
        )

    for o in range(1, n_head):
        stat(me_h, o, lax.rem(me_h + o, n_head)).start()
    for o in range(1, n_head):
        stat(lax.rem(me_h + o, n_head), o, me_h).wait_recv()
    tot = sall[0]
    for s in range(1, n_head):
        tot = tot + sall[s]
    inv = 1.0 / jnp.sqrt(tot[0:pairs] / width + 1e-06)
    coef = tot[pairs : 2 * pairs] / width * (inv * inv * inv)
    for p in range(pairs):
        r = slice(p * PAIR, (p + 1) * PAIR)
        invs[r, :] = jnp.broadcast_to(inv[p : p + 1], (PAIR, D)).T
        coefs[r, :] = jnp.broadcast_to(coef[p : p + 1], (PAIR, D)).T

    def normalise(h, carry):
        c = cols(h)
        gain = gain_ref[pl.ds(h, 1), :]
        m = mixed[:, c]
        g = og[:, c].astype(jnp.float32)
        iv = invs[...]
        mi = m * iv
        normed[:, c] = (gain * mi).astype(jnp.bfloat16)
        grad[:, c] = (gain * g * iv - m * coefs[...]).astype(jnp.bfloat16)
        gall[pos, pl.ds(h, 1), :] = jnp.sum(g * mi, axis=0, keepdims=True)
        return carry

    lax.fori_loop(0, heads, normalise, 0)

    def share(slot, o, to):
        return pltpu.make_async_remote_copy(
            src_ref=gall.at[slot], dst_ref=gall.at[slot],
            send_sem=gsend.at[o], recv_sem=grecv.at[slot],
            device_id=(to, me_h), device_id_type=MESH,
        )

    for o in range(1, n_ctx):
        share(pos, o, lax.rem(pos + o, n_ctx)).start()
    out_copies = [pltpu.make_async_copy(normed, normed_hbm, store_sem.at[0])]
    out_copies[0].start()

    def back(way, kv, h):
        return pltpu.make_async_remote_copy(
            src_ref=out_halo.at[way, kv, :, cols(h)],
            dst_ref=in_halo.at[way, kv, :, cols(h)],
            send_sem=bsend.at[way, kv, h],
            recv_sem=brecv.at[way, kv, h],
            device_id=((right, left)[way], me_h),
            device_id_type=MESH,
        )

    def backward(h, carry):
        c = cols(h)
        parts = []
        for p in range(pairs):
            r = pl.ds(p * PAIR, PAIR)
            w = pl.ds(p * PAIR, WINDOW)
            g = grad[r, c]
            w1, w2 = w1s[h, p], w2s[h, p]
            wg = dot(vext[w, c], g, NT)
            c1 = jnp.sum(w1 * wg, axis=0, keepdims=True)
            c2 = jnp.sum(w2 * wg, axis=0, keepdims=True)
            ds = ((w1 * (wg - c1) + w2 * (wg - c2)) * scale).astype(jnp.bfloat16)
            dvw = dot((w1 + w2).astype(jnp.bfloat16), g, NN)
            dkw = dot(ds, q[r, c], NN)
            dq[r, c] = dot(ds, kext[w, c], TN).astype(jnp.bfloat16)
            parts.append((dkw, dvw))
        for kv, own in ((0, dk), (1, dv)):
            out_halo[1, kv, :, c] = parts[0][kv][0:RIM].astype(jnp.bfloat16)
            out_halo[0, kv, :, c] = parts[-1][kv][WINDOW - RIM :].astype(jnp.bfloat16)
            for p in range(pairs):
                mid = parts[p][kv][RIM : RIM + PAIR]
                if p > 0:
                    mid = mid + parts[p - 1][kv][RIM + PAIR :]
                if p < pairs - 1:
                    mid = mid + parts[p + 1][kv][0:RIM]
                own[pl.ds(p * PAIR, PAIR), c] = mid

            @pl.when(pos < last)
            def _():
                back(0, kv, h).start()

            @pl.when(pos > 0)
            def _():
                back(1, kv, h).start()
        return carry

    lax.fori_loop(0, heads, backward, 0)
    dq_copy = pltpu.make_async_copy(dq, dq_hbm, store_sem.at[1])
    dq_copy.start()
    out_copies.append(dq_copy)

    for o in range(1, n_ctx):
        share(lax.rem(pos + o, n_ctx), o, pos).wait_recv()
    total = gall[0]
    for s in range(1, n_ctx):
        total = total + gall[s]
    gg_ref[...] = total / math.sqrt(rows * n_ctx)

    @pl.when(pos == 0)
    def _():
        in_halo[0] = jnp.zeros(in_halo.shape[1:], in_halo.dtype)

    @pl.when(pos == last)
    def _():
        in_halo[1] = jnp.zeros(in_halo.shape[1:], in_halo.dtype)

    def settle(h, carry):
        c = cols(h)
        for kv, own, out in ((0, dk, dko), (1, dv, dvo)):
            @pl.when(pos > 0)
            def _():
                back(0, kv, h).wait_recv()

            @pl.when(pos < last)
            def _():
                back(1, kv, h).wait_recv()
            out[0:RIM, c] = (own[0:RIM, c] + in_halo[0, kv, :, c].astype(jnp.float32)).astype(jnp.bfloat16)
            out[rows - RIM : rows, c] = (
                own[rows - RIM : rows, c] + in_halo[1, kv, :, c].astype(jnp.float32)
            ).astype(jnp.bfloat16)
        return carry

    lax.fori_loop(0, heads, settle, 0)
    for i, (src, dst) in enumerate(((dko, dk_hbm), (dvo, dv_hbm))):
        copy = pltpu.make_async_copy(src, dst, store_sem.at[2 + i])
        copy.start()
        out_copies.append(copy)

    mirror.wait_send()
    for o in range(1, n_head):
        stat(me_h, o, lax.rem(me_h + o, n_head)).wait_send()
    for o in range(1, n_ctx):
        share(pos, o, lax.rem(pos + o, n_ctx)).wait_send()

    def drain(h, carry):
        for kv in range(2):
            @pl.when(pos < last)
            def _():
                halo(0, kv, h).wait_send()
                back(0, kv, h).wait_send()

            @pl.when(pos > 0)
            def _():
                halo(1, kv, h).wait_send()
                back(1, kv, h).wait_send()
        return carry

    lax.fori_loop(0, heads, drain, 0)
    for copy in out_copies:
        copy.wait()


def body(query_vecs, key_vecs, value_vecs, out_grad, block_mask, norm_gain):
    n_ctx = lax.axis_size("ctx")
    n_head = lax.axis_size("head")
    rows, features = query_vecs.shape
    heads = features // D
    pairs = rows // PAIR
    ext = rows + 2 * RIM
    bf, f32 = jnp.bfloat16, jnp.float32
    dma = pltpu.SemaphoreType.DMA
    hbm = pl.BlockSpec(memory_space=pl.ANY)
    vmem = pl.BlockSpec(memory_space=pltpu.VMEM)
    big = jax.ShapeDtypeStruct((rows, features), bf)
    return pl.pallas_call(
        functools.partial(kernel, n_ctx, n_head),
        out_shape=(big, big, big, big, jax.ShapeDtypeStruct((heads, D), f32)),
        in_specs=[hbm, hbm, hbm, hbm, vmem, vmem],
        out_specs=(hbm, hbm, hbm, hbm, vmem),
        scratch_shapes=[
            pltpu.VMEM((rows, features), bf),
            pltpu.VMEM((ext, features), bf),
            pltpu.VMEM((ext, features), bf),
            pltpu.VMEM((rows, features), bf),
            pltpu.VMEM((8, 128), jnp.int32),
            pltpu.VMEM((8, 128), jnp.int32),
            pltpu.VMEM((2, pairs, WINDOW, PAIR), f32),
            pltpu.VMEM((heads, pairs, WINDOW, PAIR), f32),
            pltpu.VMEM((heads, pairs, WINDOW, PAIR), f32),
            pltpu.VMEM((rows, features), f32),
            pltpu.VMEM((rows, D), f32),
            pltpu.VMEM((rows, D), f32),
            pltpu.VMEM((n_head, 8, PAIR), f32),
            pltpu.VMEM((rows, D), f32),
            pltpu.VMEM((rows, D), f32),
            pltpu.VMEM((rows, features), bf),
            pltpu.VMEM((n_ctx, heads, D), f32),
            pltpu.VMEM((rows, features), bf),
            pltpu.VMEM((rows, features), bf),
            pltpu.VMEM((rows, features), f32),
            pltpu.VMEM((rows, features), f32),
            pltpu.VMEM((rows, features), bf),
            pltpu.VMEM((rows, features), bf),
            pltpu.VMEM((2, 2, RIM, features), bf),
            pltpu.VMEM((2, 2, RIM, features), bf),
            dma((4,)),
            dma((2, 2, heads)),
            dma((2, 2, heads)),
            dma,
            dma,
            dma((n_head,)),
            dma((n_head,)),
            dma((n_ctx,)),
            dma((n_ctx,)),
            dma((2, 2, heads)),
            dma((2, 2, heads)),
            dma((4,)),
        ],
        compiler_params=pltpu.CompilerParams(
            collective_id=0, has_side_effects=True, vmem_limit_bytes=48 * 1024 * 1024
        ),
        name="strand_attention",
    )(query_vecs, key_vecs, value_vecs, out_grad, block_mask, norm_gain)


def solution(mesh):
    tokens = P("ctx", "head")
    return jax.shard_map(
        body,
        mesh=mesh,
        in_specs=(tokens, tokens, tokens, tokens, P("ctx", None), P("head", None)),
        out_specs=(tokens, tokens, tokens, tokens, P("head", None)),
        check_vma=False,
    )
```

time: 179 us -> 44.1 us (0.25)
  local copies, waits for them, and re-layouts: 67.9 us -> 9.29 us
  blocking collectives: 50.2 us -> 0 us
  Pallas kernels: 0 us -> 33.8 us
  matrix products: 30.6 us -> 0 us
  other arithmetic: 16 us -> 0 us
  starting transfers between devices: 11.2 us -> 0 us
    psum x3 -> x0, blocking collectives: 35.8 us -> none  [the longest x1 15.2 us: body(): gain_grad = lax.psum(gain_part, 'ctx') / math.sqrt(own_rows * devices)]
    pallas_call x0 -> x1, Pallas kernels: none -> 33.8 us  [body(): pl.pallas_call(functools.partial(kernel, n_ctx, n_head), out_shape=(big,...]
    dot_general x14 -> x0, matrix products: 30.6 us -> none  [the longest x2 10.4 us: attend_backward(): jnp.einsum('ns,asr->anr', placement, stacked, precision=lax.Precision.HIG...]
    another operation x4 -> x0, local copies, waits for them, and re-layouts: 15.7 us -> none  [attend_backward(): jnp.stack([key_contributions, value_contributions])]
    all_gather x1 -> x0, blocking collectives: 14.4 us -> none  [body(): full_mask = lax.all_gather(block_mask, 'ctx', axis=0, tiled=True)]
    ppermute x4 -> x0, starting transfers between devices: 11.2 us -> none  [the longest x2 6.45 us: shifted(): return lax.ppermute(shard, axis, pairs)]
    mul x2 -> x0, local copies, waits for them, and re-layouts: 10.9 us -> none  [attend_backward(): jnp.einsum('bhqk,bqhd->bkhd', score_gradient, query_block_list, preferred...]
    transpose x2 -> x0, local copies, waits for them, and re-layouts: 10.5 us -> none  [attend_backward(): jnp.einsum('bhqk,bqhd->bkhd', rounded_values, gradient_block_list, prefer...]
  transfers between devices with their start and end apart: 4 -> 0, of which waited for: 0 -> 0; matrix products, arithmetic and copies ran while one was open for 3% -> 0% of each run, Pallas kernels for 0% -> 0%
where the time goes in v1:
time: 44.1 us; the launch traced here: 43.7 us
  Pallas kernels  33.8 us (77%)
  local copies, waits for them, and re-layouts  9.29 us (21%)
  between operations  0.66 us (1%)
    pallas_call x1, Pallas kernels, body(): pl.pallas_call(functools.partial(kernel, n_ctx, n_head), out_shape=(big,...  33.8 us
    unnamed x17, local copies, waits for them, and re-layouts  9.29 us

profile of v1, /device:TPU:4, one launch (start us, length us, event | category | flops | bytes accessed | tf_op | source)
XLA Modules:
  0.0 43.7 jit_solution(9464070884998101772)
XLA Ops:
  0.6 0.0 copy-start
  0.6 1.0 %copy-done = bf16[256,1024]{1,0:T(8,128)(2,1)S(1)} copy-done((bf16[256,1024]{1,0:T(8,128)(2,1)S(1)}, bf16[256,1024]{1,0:T(8,128)(2,1)}, u32[]{:S(2)}) %copy-start) | copy-done | bytes 524312
  1.7 0.0 copy-start.1
  1.7 1.0 %copy-done.1 = bf16[256,1024]{1,0:T(8,128)(2,1)S(1)} copy-done((bf16[256,1024]{1,0:T(8,128)(2,1)S(1)}, bf16[256,1024]{1,0:T(8,128)(2,1)}, u32[]{:S(2)}) %copy-start.1) | copy-done | bytes 524312
  2.7 0.0 copy-start.2
  2.7 1.0 %copy-done.2 = bf16[256,1024]{1,0:T(8,128)(2,1)S(1)} copy-done((bf16[256,1024]{1,0:T(8,128)(2,1)S(1)}, bf16[256,1024]{1,0:T(8,128)(2,1)}, u32[]{:S(2)}) %copy-start.2) | copy-done | bytes 524312
  3.8 0.0 copy-start.3
  3.8 1.0 %copy-done.3 = bf16[256,1024]{1,0:T(8,128)(2,1)S(1)} copy-done((bf16[256,1024]{1,0:T(8,128)(2,1)S(1)}, bf16[256,1024]{1,0:T(8,128)(2,1)}, u32[]{:S(2)}) %copy-start.3) | copy-done | bytes 524312
  4.8 0.0 copy-start.4
  4.8 0.7 %copy-done.4 = f32[8,128]{1,0:T(8,128)S(1)} copy-done((f32[8,128]{1,0:T(8,128)S(1)}, f32[8,128]{1,0:T(8,128)}, u32[]{:S(2)}) %copy-start.4) | copy-done | bytes 4120
  5.5 0.0 copy-start.5
  5.5 0.7 %copy-done.5 = s32[4,4]{1,0:T(4,128)S(1)} copy-done((s32[4,4]{1,0:T(4,128)S(1)}, s32[4,4]{1,0:T(4,128)}, u32[]{:S(2)}) %copy-start.5) | copy-done | bytes 88
  6.2 33.8 %strand_attention.1 = (bf16[256,1024]{1,0:T(8,128)(2,1)S(1)}, bf16[256,1024]{1,0:T(8,128)(2,1)S(1)}, bf16[256,1024]{1,0:T(8,128)(2,1)S(1)}, bf16[256,1024]{1,0:T(8,128)(2,1)S(1)}, f32[8,128]{1,0:T(8,128)S(1)}) custom-call(bf16[256,1024]{1,0:T(8,128)(2,1)S(1)} %copy-done, bf16[256,1024]{1,0:T(8,128)(2,1)S(1)} %copy-done.1, bf16[256,1024]{1,0:T(8,128)(2,1)S(1)} %copy-done.2, ...), custom_call_target="tpu_custom_call" | custom-call | tf_op jit(solution)/shard_map/strand_attention/pallas_call | solution.py:348
  40.0 0.8 %copy.16 = bf16[256,1024]{1,0:T(8,128)(2,1)} copy(bf16[256,1024]{1,0:T(8,128)(2,1)S(1)} %get-tuple-element.10) | data formatting | bytes 1048576
  40.8 0.8 %copy.17 = bf16[256,1024]{1,0:T(8,128)(2,1)} copy(bf16[256,1024]{1,0:T(8,128)(2,1)S(1)} %get-tuple-element.11) | data formatting | bytes 1048576
  41.6 0.8 %copy.18 = bf16[256,1024]{1,0:T(8,128)(2,1)} copy(bf16[256,1024]{1,0:T(8,128)(2,1)S(1)} %get-tuple-element.12) | data formatting | bytes 1048576
  42.3 0.8 %copy.19 = bf16[256,1024]{1,0:T(8,128)(2,1)} copy(bf16[256,1024]{1,0:T(8,128)(2,1)S(1)} %get-tuple-element.13) | data formatting | bytes 1048576
  43.1 0.6 %copy.20 = f32[8,128]{1,0:T(8,128)} copy(f32[8,128]{1,0:T(8,128)S(1)} %get-tuple-element.14) | data formatting | bytes 8192
Async XLA Ops:
  0.6 1.0 %copy-start = (bf16[256,1024]{1,0:T(8,128)(2,1)S(1)}, bf16[256,1024]{1,0:T(8,128)(2,1)}, u32[]{:S(2)}) copy-start(bf16[256,1024]{1,0:T(8,128)(2,1)} %q_hbm.1) | copy-start | bytes 1572868
  1.7 1.0 %copy-start.1 = (bf16[256,1024]{1,0:T(8,128)(2,1)S(1)}, bf16[256,1024]{1,0:T(8,128)(2,1)}, u32[]{:S(2)}) copy-start(bf16[256,1024]{1,0:T(8,128)(2,1)} %k_hbm.1) | copy-start | bytes 1572868
  2.7 1.0 %copy-start.2 = (bf16[256,1024]{1,0:T(8,128)(2,1)S(1)}, bf16[256,1024]{1,0:T(8,128)(2,1)}, u32[]{:S(2)}) copy-start(bf16[256,1024]{1,0:T(8,128)(2,1)} %v_hbm.1) | copy-start | bytes 1572868
  3.8 1.0 %copy-start.3 = (bf16[256,1024]{1,0:T(8,128)(2,1)S(1)}, bf16[256,1024]{1,0:T(8,128)(2,1)}, u32[]{:S(2)}) copy-start(bf16[256,1024]{1,0:T(8,128)(2,1)} %og_hbm.1) | copy-start | bytes 1572868
  4.8 0.7 %copy-start.4 = (f32[8,128]{1,0:T(8,128)S(1)}, f32[8,128]{1,0:T(8,128)}, u32[]{:S(2)}) copy-start(f32[8,128]{1,0:T(8,128)} %gain_ref.1) | copy-start | bytes 12292
  5.5 0.7 %copy-start.5 = (s32[4,4]{1,0:T(4,128)S(1)}, s32[4,4]{1,0:T(4,128)}, u32[]{:S(2)}) copy-start(s32[4,4]{1,0:T(4,128)} %mask_ref.1) | copy-start | bytes 196

commit v2 on v1

--- a/solution.py
+++ b/solution.py
@@ -14,6 +14,7 @@
 RIM = BAND * BLOCK
 PAIR = 2 * BLOCK
 WINDOW = PAIR + 2 * RIM
+VMEM = 64 * 1024 * 1024
 MESH = pl.DeviceIdType.MESH
 NT = (((1,), (1,)), ((), ()))
 TN = (((0,), (0,)), ((), ()))
@@ -26,9 +27,9 @@
 
 def kernel(
     n_ctx, n_head,
-    q_hbm, k_hbm, v_hbm, og_hbm, mask_ref, gain_ref,
+    q_hbm, k_hbm, v_hbm, og_hbm, mask_hbm, gain_hbm,
     normed_hbm, dq_hbm, dk_hbm, dv_hbm, gg_ref,
-    q, kext, vext, og, mine, theirs, bias, w1s, w2s, mixed, sq, inner, sall, invs, coefs,
+    mask_ref, gain_ref, q, kext, vext, og, mine, theirs, bias, w1s, w2s, mixed, sq, inner, sall, invs, coefs,
     grad, gall, normed, dq, dk, dv, dko, dvo, out_halo, in_halo,
     load_sem, fsend, frecv, msend, mrecv, ssend, srecv, gsend, grecv, bsend, brecv, store_sem,
 ):
@@ -42,13 +43,17 @@
     scale = D ** -0.5
     last = n_ctx - 1
 
+    small = [
+        pltpu.make_async_copy(mask_hbm, mask_ref, load_sem.at[4]),
+        pltpu.make_async_copy(gain_hbm, gain_ref, load_sem.at[5]),
+    ]
     loads = [
         pltpu.make_async_copy(k_hbm, kext.at[pl.ds(RIM, rows)], load_sem.at[0]),
         pltpu.make_async_copy(q_hbm, q, load_sem.at[1]),
         pltpu.make_async_copy(v_hbm, vext.at[pl.ds(RIM, rows)], load_sem.at[2]),
         pltpu.make_async_copy(og_hbm, og, load_sem.at[3]),
     ]
-    for copy in loads:
+    for copy in small + loads:
         copy.start()
 
     barrier = pltpu.get_barrier_semaphore()
@@ -57,6 +62,8 @@
     for o in range(1, n_head):
         pl.semaphore_signal(barrier, inc=1, device_id=(pos, lax.rem(me_h + o, n_head)), device_id_type=MESH)
     mine[...] = jnp.zeros_like(mine)
+    for copy in small:
+        copy.wait()
     mine[0:blocks_dev, 0:mask_ref.shape[1]] = mask_ref[...]
     sall[me_h] = jnp.zeros(sall.shape[1:], jnp.float32)
     sq[...] = jnp.zeros_like(sq)
@@ -333,6 +340,16 @@
         copy.wait()
 
 
+def store_kernel(*refs):
+    count = len(refs) // 2
+    sems = refs[-1]
+    copies = [pltpu.make_async_copy(refs[i], refs[count + i], sems.at[i]) for i in range(count)]
+    for copy in copies:
+        copy.start()
+    for copy in copies:
+        copy.wait()
+
+
 def body(query_vecs, key_vecs, value_vecs, out_grad, block_mask, norm_gain):
     n_ctx = lax.axis_size("ctx")
     n_head = lax.axis_size("head")
@@ -344,13 +361,16 @@
     dma = pltpu.SemaphoreType.DMA
     hbm = pl.BlockSpec(memory_space=pl.ANY)
     vmem = pl.BlockSpec(memory_space=pltpu.VMEM)
+    fixed = pl.BlockSpec(memory_space=pltpu.HBM)
     big = jax.ShapeDtypeStruct((rows, features), bf)
-    return pl.pallas_call(
+    results = pl.pallas_call(
         functools.partial(kernel, n_ctx, n_head),
         out_shape=(big, big, big, big, jax.ShapeDtypeStruct((heads, D), f32)),
-        in_specs=[hbm, hbm, hbm, hbm, vmem, vmem],
+        in_specs=[fixed] * 6,
         out_specs=(hbm, hbm, hbm, hbm, vmem),
         scratch_shapes=[
+            pltpu.VMEM(block_mask.shape, jnp.int32),
+            pltpu.VMEM(norm_gain.shape, f32),
             pltpu.VMEM((rows, features), bf),
             pltpu.VMEM((ext, features), bf),
             pltpu.VMEM((ext, features), bf),
@@ -376,7 +396,7 @@
             pltpu.VMEM((rows, features), bf),
             pltpu.VMEM((2, 2, RIM, features), bf),
             pltpu.VMEM((2, 2, RIM, features), bf),
-            dma((4,)),
+            dma((6,)),
             dma((2, 2, heads)),
             dma((2, 2, heads)),
             dma,
@@ -390,10 +410,19 @@
             dma((4,)),
         ],
         compiler_params=pltpu.CompilerParams(
-            collective_id=0, has_side_effects=True, vmem_limit_bytes=48 * 1024 * 1024
+            collective_id=0, has_side_effects=True, vmem_limit_bytes=VMEM
         ),
         name="strand_attention",
     )(query_vecs, key_vecs, value_vecs, out_grad, block_mask, norm_gain)
+    return pl.pallas_call(
+        store_kernel,
+        out_shape=tuple(jax.ShapeDtypeStruct(x.shape, x.dtype) for x in results),
+        in_specs=[hbm] * 5,
+        out_specs=(fixed,) * 5,
+        scratch_shapes=[dma((5,))],
+        compiler_params=pltpu.CompilerParams(vmem_limit_bytes=VMEM),
+        name="store_results",
+    )(*results)
 
 
 def solution(mesh):

time: 44.1 us -> 101 us (2.29)
  Pallas kernels: 33.8 us -> 100 us
  local copies, waits for them, and re-layouts: 9.29 us -> 0 us
    pallas_call x0 -> x1, Pallas kernels: none -> 64.8 us  [body(): pl.pallas_call(store_kernel, out_shape=tuple((jax.ShapeDtypeStruct(x.shap...]
    unnamed x17 -> x0, local copies, waits for them, and re-layouts: 9.29 us -> none
    pallas_call x1, Pallas kernels: 33.8 us -> 35.2 us  [body(): pl.pallas_call(functools.partial(kernel, n_ctx, n_head), out_shape=(big,...]
where the time goes in v2:
time: 101 us
  Pallas kernels  100 us (99%)
    pallas_call x1, Pallas kernels, body(): pl.pallas_call(store_kernel, out_shape=tuple((jax.ShapeDtypeStruct(x.shap...  64.8 us
    pallas_call x1, Pallas kernels, body(): pl.pallas_call(functools.partial(kernel, n_ctx, n_head), out_shape=(big,...  35.2 us

profile of v2, /device:TPU:4, one launch (start us, length us, event | category | flops | bytes accessed | tf_op | source)
XLA Modules:
  0.0 100.7 jit_solution(7436454346876278358)
XLA Ops:
  0.6 35.2 %strand_attention.1 = (bf16[256,1024]{1,0:T(8,128)(2,1)}, bf16[256,1024]{1,0:T(8,128)(2,1)}, bf16[256,1024]{1,0:T(8,128)(2,1)}, bf16[256,1024]{1,0:T(8,128)(2,1)}, f32[8,128]{1,0:T(8,128)}) custom-call(bf16[256,1024]{1,0:T(8,128)(2,1)} %q_hbm.1, bf16[256,1024]{1,0:T(8,128)(2,1)} %k_hbm.1, bf16[256,1024]{1,0:T(8,128)(2,1)} %v_hbm.1, ...), custom_call_target="tpu_custom_call" | custom-call | tf_op jit(solution)/shard_map/strand_attention/pallas_call | solution.py:366
  35.9 64.8 %store_results.1 = (bf16[256,1024]{1,0:T(8,128)(2,1)}, bf16[256,1024]{1,0:T(8,128)(2,1)}, bf16[256,1024]{1,0:T(8,128)(2,1)}, bf16[256,1024]{1,0:T(8,128)(2,1)}, f32[8,128]{1,0:T(8,128)}) custom-call(bf16[256,1024]{1,0:T(8,128)(2,1)} %get-tuple-element.10.refs_0_, bf16[256,1024]{1,0:T(8,128)(2,1)} %get-tuple-element.11.refs_1_, ...), custom_call_target="tpu_custom_call" | custom-call | tf_op jit(solution)/shard_map/store_results/pallas_call | solution.py:417

commit v3 on v2

--- a/solution.py
+++ b/solution.py
@@ -15,6 +15,7 @@
 PAIR = 2 * BLOCK
 WINDOW = PAIR + 2 * RIM
 VMEM = 64 * 1024 * 1024
+GROUP = 2
 MESH = pl.DeviceIdType.MESH
 NT = (((1,), (1,)), ((), ()))
 TN = (((0,), (0,)), ((), ()))
@@ -146,35 +147,40 @@
     for copy in loads:
         copy.wait()
 
-    def forward(h, carry):
-        c = cols(h)
-        for kv in range(2):
-            @pl.when(pos > 0)
-            def _():
-                halo(0, kv, h).wait_recv()
-
-            @pl.when(pos < last)
-            def _():
-                halo(1, kv, h).wait_recv()
-        gain = gain_ref[pl.ds(h, 1), :]
+    def forward(step, carry):
+        group = [step * GROUP + i for i in range(GROUP)]
+        for h in group:
+            for kv in range(2):
+                @pl.when(pos > 0)
+                def _():
+                    halo(0, kv, h).wait_recv()
+
+                @pl.when(pos < last)
+                def _():
+                    halo(1, kv, h).wait_recv()
         for p in range(pairs):
             r = pl.ds(p * PAIR, PAIR)
             w = pl.ds(p * PAIR, WINDOW)
-            scores = dot(kext[w, c], q[r, c], NT) * scale
-            total = None
-            for strand, kept in ((0, w1s), (1, w2s)):
-                s = scores + bias[strand, p]
-                e = jnp.exp(s - jnp.max(s, axis=0, keepdims=True))
-                e = e * (1.0 / jnp.sum(e, axis=0, keepdims=True))
-                kept[h, p] = e
-                total = e if total is None else total + e
-            m = dot(total.astype(jnp.bfloat16), vext[w, c], TN)
-            mixed[r, c] = m
-            sq[r, :] += m * m
-            inner[r, :] += gain * og[r, c].astype(jnp.float32) * m
-        return carry
-
-    lax.fori_loop(0, heads, forward, 0)
+            squares, products = sq[r, :], inner[r, :]
+            for h in group:
+                c = cols(h)
+                scores = dot(kext[w, c], q[r, c], NT) * scale
+                total = None
+                for strand, kept in ((0, w1s), (1, w2s)):
+                    s = scores + bias[strand, p]
+                    e = jnp.exp(s - jnp.max(s, axis=0, keepdims=True))
+                    e = e * (1.0 / jnp.sum(e, axis=0, keepdims=True))
+                    kept[h, p] = e
+                    total = e if total is None else total + e
+                m = dot(total.astype(jnp.bfloat16), vext[w, c], TN)
+                mixed[r, c] = m
+                squares = squares + m * m
+                products = products + gain_ref[pl.ds(h, 1), :] * og[r, c].astype(jnp.float32) * m
+            sq[r, :] = squares
+            inner[r, :] = products
+        return carry
+
+    lax.fori_loop(0, heads // GROUP, forward, 0)
 
     for p in range(pairs):
         r = slice(p * PAIR, (p + 1) * PAIR)
@@ -238,43 +244,46 @@
             device_id_type=MESH,
         )
 
-    def backward(h, carry):
-        c = cols(h)
-        parts = []
-        for p in range(pairs):
-            r = pl.ds(p * PAIR, PAIR)
-            w = pl.ds(p * PAIR, WINDOW)
-            g = grad[r, c]
-            w1, w2 = w1s[h, p], w2s[h, p]
-            wg = dot(vext[w, c], g, NT)
-            c1 = jnp.sum(w1 * wg, axis=0, keepdims=True)
-            c2 = jnp.sum(w2 * wg, axis=0, keepdims=True)
-            ds = ((w1 * (wg - c1) + w2 * (wg - c2)) * scale).astype(jnp.bfloat16)
-            dvw = dot((w1 + w2).astype(jnp.bfloat16), g, NN)
-            dkw = dot(ds, q[r, c], NN)
-            dq[r, c] = dot(ds, kext[w, c], TN).astype(jnp.bfloat16)
-            parts.append((dkw, dvw))
-        for kv, own in ((0, dk), (1, dv)):
-            out_halo[1, kv, :, c] = parts[0][kv][0:RIM].astype(jnp.bfloat16)
-            out_halo[0, kv, :, c] = parts[-1][kv][WINDOW - RIM :].astype(jnp.bfloat16)
+    def backward(step, carry):
+        group = [step * GROUP + i for i in range(GROUP)]
+        for h in group:
+            c = cols(h)
+            parts = []
             for p in range(pairs):
-                mid = parts[p][kv][RIM : RIM + PAIR]
-                if p > 0:
-                    mid = mid + parts[p - 1][kv][RIM + PAIR :]
-                if p < pairs - 1:
-                    mid = mid + parts[p + 1][kv][0:RIM]
-                own[pl.ds(p * PAIR, PAIR), c] = mid
-
-            @pl.when(pos < last)
-            def _():
-                back(0, kv, h).start()
-
-            @pl.when(pos > 0)
-            def _():
-                back(1, kv, h).start()
-        return carry
-
-    lax.fori_loop(0, heads, backward, 0)
+                r = pl.ds(p * PAIR, PAIR)
+                w = pl.ds(p * PAIR, WINDOW)
+                g = grad[r, c]
+                w1, w2 = w1s[h, p], w2s[h, p]
+                wg = dot(vext[w, c], g, NT)
+                c1 = jnp.sum(w1 * wg, axis=0, keepdims=True)
+                c2 = jnp.sum(w2 * wg, axis=0, keepdims=True)
+                ds = ((w1 * (wg - c1) + w2 * (wg - c2)) * scale).astype(jnp.bfloat16)
+                dvw = dot((w1 + w2).astype(jnp.bfloat16), g, NN)
+                dkw = dot(ds, q[r, c], NN)
+                dq[r, c] = dot(ds, kext[w, c], TN).astype(jnp.bfloat16)
+                parts.append((dkw, dvw))
+            for kv, own in ((0, dk), (1, dv)):
+                out_halo[1, kv, :, c] = parts[0][kv][0:RIM].astype(jnp.bfloat16)
+                out_halo[0, kv, :, c] = parts[-1][kv][WINDOW - RIM :].astype(jnp.bfloat16)
+                for p in range(pairs):
+                    mid = parts[p][kv][RIM : RIM + PAIR]
+                    if p > 0:
+                        mid = mid + parts[p - 1][kv][RIM + PAIR :]
+                    if p < pairs - 1:
+                        mid = mid + parts[p + 1][kv][0:RIM]
+                    own[pl.ds(p * PAIR, PAIR), c] = mid
+        for h in group:
+            for kv in range(2):
+                @pl.when(pos < last)
+                def _():
+                    back(0, kv, h).start()
+
+                @pl.when(pos > 0)
+                def _():
+                    back(1, kv, h).start()
+        return carry
+
+    lax.fori_loop(0, heads // GROUP, backward, 0)
     dq_copy = pltpu.make_async_copy(dq, dq_hbm, store_sem.at[1])
     dq_copy.start()
     out_copies.append(dq_copy)
@@ -341,12 +350,17 @@
 
 
 def store_kernel(*refs):
-    count = len(refs) // 2
-    sems = refs[-1]
-    copies = [pltpu.make_async_copy(refs[i], refs[count + i], sems.at[i]) for i in range(count)]
-    for copy in copies:
+    count = (len(refs) - 2) // 3
+    ins, outs, held = refs[:count], refs[count : 2 * count], refs[2 * count : 3 * count]
+    load_sem, store_sem = refs[3 * count :]
+    loads = [pltpu.make_async_copy(ins[i], held[i], load_sem.at[i]) for i in range(count)]
+    stores = [pltpu.make_async_copy(held[i], outs[i], store_sem.at[i]) for i in range(count)]
+    for copy in loads:
         copy.start()
-    for copy in copies:
+    for load, store in zip(loads, stores):
+        load.wait()
+        store.start()
+    for copy in stores:
         copy.wait()
 
 
@@ -419,7 +433,7 @@
         out_shape=tuple(jax.ShapeDtypeStruct(x.shape, x.dtype) for x in results),
         in_specs=[hbm] * 5,
         out_specs=(fixed,) * 5,
-        scratch_shapes=[dma((5,))],
+        scratch_shapes=[pltpu.VMEM(x.shape, x.dtype) for x in results] + [dma((5,)), dma((5,))],
         compiler_params=pltpu.CompilerParams(vmem_limit_bytes=VMEM),
         name="store_results",
     )(*results)

time: 101 us -> 39.1 us (0.39)
  Pallas kernels: 100 us -> 38.3 us
    pallas_call x1, Pallas kernels: 64.8 us -> 2.44 us  [body(): pl.pallas_call(store_kernel, out_shape=tuple((jax.ShapeDtypeStruct(x.shap...]
where the time goes in v3:
time: 39.1 us; the launch traced here: 38.9 us
  Pallas kernels  38.3 us (98%)
  between operations  0.64 us (2%)
    pallas_call x1, Pallas kernels, body(): pl.pallas_call(functools.partial(kernel, n_ctx, n_head), out_shape=(big,...  35.9 us
    pallas_call x1, Pallas kernels, body(): pl.pallas_call(store_kernel, out_shape=tuple((jax.ShapeDtypeStruct(x.shap...  2.44 us

profile of v3, /device:TPU:4, one launch (start us, length us, event | category | flops | bytes accessed | tf_op | source)
XLA Modules:
  0.0 38.9 jit_solution(13996463338435897249)
XLA Ops:
  0.6 35.9 %strand_attention.1 = (bf16[256,1024]{1,0:T(8,128)(2,1)}, bf16[256,1024]{1,0:T(8,128)(2,1)}, bf16[256,1024]{1,0:T(8,128)(2,1)}, bf16[256,1024]{1,0:T(8,128)(2,1)}, f32[8,128]{1,0:T(8,128)}) custom-call(bf16[256,1024]{1,0:T(8,128)(2,1)} %q_hbm.1, bf16[256,1024]{1,0:T(8,128)(2,1)} %k_hbm.1, bf16[256,1024]{1,0:T(8,128)(2,1)} %v_hbm.1, ...), custom_call_target="tpu_custom_call" | custom-call | tf_op jit(solution)/shard_map/strand_attention/pallas_call | solution.py:380
  36.5 2.4 %store_results.1 = (bf16[256,1024]{1,0:T(8,128)(2,1)}, bf16[256,1024]{1,0:T(8,128)(2,1)}, bf16[256,1024]{1,0:T(8,128)(2,1)}, bf16[256,1024]{1,0:T(8,128)(2,1)}, f32[8,128]{1,0:T(8,128)}) custom-call(bf16[256,1024]{1,0:T(8,128)(2,1)} %get-tuple-element.10.refs_0_, bf16[256,1024]{1,0:T(8,128)(2,1)} %get-tuple-element.11.refs_1_, ...), custom_call_target="tpu_custom_call" | custom-call | tf_op jit(solution)/shard_map/store_results/pallas_call | solution.py:431

commit v4 on v3

--- a/solution.py
+++ b/solution.py
@@ -32,7 +32,7 @@
     normed_hbm, dq_hbm, dk_hbm, dv_hbm, gg_ref,
     mask_ref, gain_ref, q, kext, vext, og, mine, theirs, bias, w1s, w2s, mixed, sq, inner, sall, invs, coefs,
     grad, gall, normed, dq, dk, dv, dko, dvo, out_halo, in_halo,
-    load_sem, fsend, frecv, msend, mrecv, ssend, srecv, gsend, grecv, bsend, brecv, store_sem,
+    load_sem, fsend, frecv, msend, mrecv, ssend, srecv, gsend, grecv, bsend, brecv, store_sem, relay, asend, rsend, rrecv,
 ):
     pos = lax.axis_index("ctx")
     me_h = lax.axis_index("head")
@@ -88,6 +88,62 @@
     right = jnp.minimum(pos + 1, last)
     left = jnp.maximum(pos - 1, 0)
 
+    square = n_ctx == 8
+    ends = (n_ctx // 2 - 1, n_ctx // 2)
+    corners = (last, 0)
+
+    def first_leg(way, phase, kv, step):
+        h = step * GROUP + 1
+        if phase == 0:
+            src = (k_hbm, v_hbm)[kv].at[pl.ds((rows - RIM, 0)[way], RIM), cols(h)]
+        else:
+            src = out_halo.at[way, kv, :, cols(h)]
+        return pltpu.make_async_remote_copy(
+            src_ref=src, dst_ref=relay.at[phase, kv, step],
+            send_sem=asend.at[phase, kv, step], recv_sem=rrecv.at[phase, kv, step],
+            device_id=(corners[way], me_h), device_id_type=MESH,
+        )
+
+    def second_leg(way, phase, kv, step):
+        h = step * GROUP + 1
+        if phase == 0:
+            dst = (kext, vext)[kv].at[pl.ds((0, rows + RIM)[way], RIM), cols(h)]
+            sem = frecv.at[way, kv, h]
+        else:
+            dst = in_halo.at[way, kv, :, cols(h)]
+            sem = brecv.at[way, kv, h]
+        return pltpu.make_async_remote_copy(
+            src_ref=relay.at[phase, kv, step], dst_ref=dst,
+            send_sem=rsend.at[phase, kv, step], recv_sem=sem,
+            device_id=(ends[1 - way], me_h), device_id_type=MESH,
+        )
+
+    def pass_on(phase, step):
+        if square:
+            for way in range(2):
+                @pl.when(pos == corners[way])
+                def _():
+                    for kv in range(2):
+                        first_leg(way, phase, kv, step).wait_recv()
+                        second_leg(way, phase, kv, step).start()
+
+    def each_send(phase, step, plain, act):
+        for i in range(GROUP):
+            h = step * GROUP + i
+            for kv in range(2):
+                for way in range(2):
+                    able = (pos < last, pos > 0)[way]
+                    if square and i == 1:
+                        @pl.when(pos == ends[way])
+                        def _():
+                            act(first_leg(way, phase, kv, step))
+
+                        able = able & (pos != ends[way])
+
+                    @pl.when(able)
+                    def _():
+                        act(plain(way, kv, h))
+
     def halo(way, kv, h):
         src = (k_hbm, v_hbm)[kv]
         dst = (kext, vext)[kv]
@@ -107,18 +163,11 @@
     )
     mirror.start()
 
-    def send_halos(h, carry):
-        for kv in range(2):
-            @pl.when(pos < last)
-            def _():
-                halo(0, kv, h).start()
-
-            @pl.when(pos > 0)
-            def _():
-                halo(1, kv, h).start()
+    def send_halos(step, carry):
+        each_send(0, step, halo, lambda copy: copy.start())
         return carry
 
-    lax.fori_loop(0, heads, send_halos, 0)
+    lax.fori_loop(0, heads // GROUP, send_halos, 0)
     mirror.wait_recv()
 
     all_blocks = blocks_dev * n_ctx
@@ -149,6 +198,7 @@
 
     def forward(step, carry):
         group = [step * GROUP + i for i in range(GROUP)]
+        pass_on(0, step)
         for h in group:
             for kv in range(2):
                 @pl.when(pos > 0)
@@ -272,18 +322,16 @@
                     if p < pairs - 1:
                         mid = mid + parts[p + 1][kv][0:RIM]
                     own[pl.ds(p * PAIR, PAIR), c] = mid
-        for h in group:
-            for kv in range(2):
-                @pl.when(pos < last)
-                def _():
-                    back(0, kv, h).start()
-
-                @pl.when(pos > 0)
-                def _():
-                    back(1, kv, h).start()
+        each_send(1, step, back, lambda copy: copy.start())
+
+        @pl.when(step > 0)
+        def _():
+            pass_on(1, step - 1)
+
         return carry
 
     lax.fori_loop(0, heads // GROUP, backward, 0)
+    pass_on(1, heads // GROUP - 1)
     dq_copy = pltpu.make_async_copy(dq, dq_hbm, store_sem.at[1])
     dq_copy.start()
     out_copies.append(dq_copy)
@@ -331,20 +379,18 @@
     for o in range(1, n_ctx):
         share(pos, o, lax.rem(pos + o, n_ctx)).wait_send()
 
-    def drain(h, carry):
-        for kv in range(2):
-            @pl.when(pos < last)
-            def _():
-                halo(0, kv, h).wait_send()
-                back(0, kv, h).wait_send()
-
-            @pl.when(pos > 0)
-            def _():
-                halo(1, kv, h).wait_send()
-                back(1, kv, h).wait_send()
+    def drain(step, carry):
+        for phase, plain in ((0, halo), (1, back)):
+            each_send(phase, step, plain, lambda copy: copy.wait_send())
+            if square:
+                for way in range(2):
+                    @pl.when(pos == corners[way])
+                    def _():
+                        for kv in range(2):
+                            second_leg(way, phase, kv, step).wait_send()
         return carry
 
-    lax.fori_loop(0, heads, drain, 0)
+    lax.fori_loop(0, heads // GROUP, drain, 0)
     for copy in out_copies:
         copy.wait()
 
@@ -422,6 +468,10 @@
             dma((2, 2, heads)),
             dma((2, 2, heads)),
             dma((4,)),
+            pltpu.VMEM((2, 2, heads // GROUP, RIM, D), bf),
+            dma((2, 2, heads // GROUP)),
+            dma((2, 2, heads // GROUP)),
+            dma((2, 2, heads // GROUP)),
         ],
         compiler_params=pltpu.CompilerParams(
             collective_id=0, has_side_effects=True, vmem_limit_bytes=VMEM

time: 39.1 us -> 39.2 us (level)
  the two profiles are of different devices: /device:TPU:4 before, /device:TPU:1 now
where the time goes in v4:
time: 39.2 us; the launch traced here: 39.1 us
  Pallas kernels  38.4 us (98%)
  between operations  0.64 us (2%)
    pallas_call x1, Pallas kernels, body(): pl.pallas_call(functools.partial(kernel, n_ctx, n_head), out_shape=(big,...  36 us
    pallas_call x1, Pallas kernels, body(): pl.pallas_call(store_kernel, out_shape=tuple((jax.ShapeDtypeStruct(x.shap...  2.44 us

profile of v4, /device:TPU:1, one launch (start us, length us, event | category | flops | bytes accessed | tf_op | source)
XLA Modules:
  0.0 39.1 jit_solution(8191056319655175708)
XLA Ops:
  0.6 36.0 %strand_attention.1 = (bf16[256,1024]{1,0:T(8,128)(2,1)}, bf16[256,1024]{1,0:T(8,128)(2,1)}, bf16[256,1024]{1,0:T(8,128)(2,1)}, bf16[256,1024]{1,0:T(8,128)(2,1)}, f32[8,128]{1,0:T(8,128)}) custom-call(bf16[256,1024]{1,0:T(8,128)(2,1)} %q_hbm.1, bf16[256,1024]{1,0:T(8,128)(2,1)} %k_hbm.1, bf16[256,1024]{1,0:T(8,128)(2,1)} %v_hbm.1, ...), custom_call_target="tpu_custom_call" | custom-call | tf_op jit(solution)/shard_map/strand_attention/pallas_call | solution.py:426
  36.6 2.4 %store_results.1 = (bf16[256,1024]{1,0:T(8,128)(2,1)}, bf16[256,1024]{1,0:T(8,128)(2,1)}, bf16[256,1024]{1,0:T(8,128)(2,1)}, bf16[256,1024]{1,0:T(8,128)(2,1)}, f32[8,128]{1,0:T(8,128)}) custom-call(bf16[256,1024]{1,0:T(8,128)(2,1)} %get-tuple-element.10.refs_0_, bf16[256,1024]{1,0:T(8,128)(2,1)} %get-tuple-element.11.refs_1_, ...), custom_call_target="tpu_custom_call" | custom-call | tf_op jit(solution)/shard_map/store_results/pallas_call | solution.py:481

commit v5 on v3

--- a/solution.py
+++ b/solution.py
@@ -30,9 +30,9 @@
     n_ctx, n_head,
     q_hbm, k_hbm, v_hbm, og_hbm, mask_hbm, gain_hbm,
     normed_hbm, dq_hbm, dk_hbm, dv_hbm, gg_ref,
-    mask_ref, gain_ref, q, kext, vext, og, mine, theirs, bias, w1s, w2s, mixed, sq, inner, sall, invs, coefs,
+    mask_ref, gain_ref, q, kvext, og, mine, theirs, bias, w1s, w2s, mixed, sq, inner, sall, invs, coefs,
     grad, gall, normed, dq, dk, dv, dko, dvo, out_halo, in_halo,
-    load_sem, fsend, frecv, msend, mrecv, ssend, srecv, gsend, grecv, bsend, brecv, store_sem,
+    load_sem, fsend, frecv, msend, mrecv, ssend, srecv, gsend, grecv, bsend, brecv, store_sem, kv_sem,
 ):
     pos = lax.axis_index("ctx")
     me_h = lax.axis_index("head")
@@ -45,16 +45,23 @@
     last = n_ctx - 1
 
     small = [
-        pltpu.make_async_copy(mask_hbm, mask_ref, load_sem.at[4]),
-        pltpu.make_async_copy(gain_hbm, gain_ref, load_sem.at[5]),
+        pltpu.make_async_copy(mask_hbm, mask_ref, load_sem.at[2]),
+        pltpu.make_async_copy(gain_hbm, gain_ref, load_sem.at[3]),
     ]
+    def cols(h):
+        return pl.ds(pl.multiple_of(h * D, D), D)
+
+    def head_load(kv, h):
+        return pltpu.make_async_copy(
+            (k_hbm, v_hbm)[kv].at[:, cols(h)], kvext.at[h, kv, pl.ds(RIM, rows)], kv_sem.at[kv, h]
+        )
+
     loads = [
-        pltpu.make_async_copy(k_hbm, kext.at[pl.ds(RIM, rows)], load_sem.at[0]),
-        pltpu.make_async_copy(q_hbm, q, load_sem.at[1]),
-        pltpu.make_async_copy(v_hbm, vext.at[pl.ds(RIM, rows)], load_sem.at[2]),
-        pltpu.make_async_copy(og_hbm, og, load_sem.at[3]),
+        pltpu.make_async_copy(q_hbm, q, load_sem.at[0]),
+        pltpu.make_async_copy(og_hbm, og, load_sem.at[1]),
     ]
-    for copy in small + loads:
+    kv_loads = [head_load(kv, h) for h in range(heads) for kv in range(2)]
+    for copy in small + kv_loads + loads:
         copy.start()
 
     barrier = pltpu.get_barrier_semaphore()
@@ -72,31 +79,24 @@
 
     @pl.when(pos == 0)
     def _():
-        kext[0:RIM, :] = jnp.zeros((RIM, features), kext.dtype)
-        vext[0:RIM, :] = jnp.zeros((RIM, features), vext.dtype)
+        kvext[:, :, 0:RIM, :] = jnp.zeros((heads, 2, RIM, D), kvext.dtype)
 
     @pl.when(pos == last)
     def _():
-        kext[rows + RIM :, :] = jnp.zeros((RIM, features), kext.dtype)
-        vext[rows + RIM :, :] = jnp.zeros((RIM, features), vext.dtype)
+        kvext[:, :, rows + RIM :, :] = jnp.zeros((heads, 2, RIM, D), kvext.dtype)
 
     pl.semaphore_wait(barrier, n_ctx - 1 + n_head - 1)
-
-    def cols(h):
-        return pl.ds(pl.multiple_of(h * D, D), D)
 
     right = jnp.minimum(pos + 1, last)
     left = jnp.maximum(pos - 1, 0)
 
-    def halo(way, kv, h):
-        src = (k_hbm, v_hbm)[kv]
-        dst = (kext, vext)[kv]
-        from_row, to_row = ((rows - RIM, 0), (0, rows + RIM))[way]
+    def halo(way, h):
+        from_row, to_row = ((rows, 0), (RIM, rows + RIM))[way]
         return pltpu.make_async_remote_copy(
-            src_ref=src.at[pl.ds(from_row, RIM), cols(h)],
-            dst_ref=dst.at[pl.ds(to_row, RIM), cols(h)],
-            send_sem=fsend.at[way, kv, h],
-            recv_sem=frecv.at[way, kv, h],
+            src_ref=kvext.at[h, :, pl.ds(from_row, RIM)],
+            dst_ref=kvext.at[h, :, pl.ds(to_row, RIM)],
+            send_sem=fsend.at[way, h],
+            recv_sem=frecv.at[way, h],
             device_id=((right, left)[way], me_h),
             device_id_type=MESH,
         )
@@ -107,18 +107,29 @@
     )
     mirror.start()
 
-    def send_halos(h, carry):
-        for kv in range(2):
-            @pl.when(pos < last)
-            def _():
-                halo(0, kv, h).start()
-
-            @pl.when(pos > 0)
-            def _():
-                halo(1, kv, h).start()
-        return carry
-
-    lax.fori_loop(0, heads, send_halos, 0)
+    for copy in kv_loads:
+        copy.wait()
+
+    def each_way(act, plain, h):
+        @pl.when(pos < last)
+        def _():
+            act(plain(0, h))
+
+        @pl.when(pos > 0)
+        def _():
+            act(plain(1, h))
+
+    def each_arrival(plain, h):
+        @pl.when(pos > 0)
+        def _():
+            plain(0, h).wait_recv()
+
+        @pl.when(pos < last)
+        def _():
+            plain(1, h).wait_recv()
+
+    for h in range(heads):
+        each_way(lambda copy: copy.start(), halo, h)
     mirror.wait_recv()
 
     all_blocks = blocks_dev * n_ctx
@@ -150,21 +161,14 @@
     def forward(step, carry):
         group = [step * GROUP + i for i in range(GROUP)]
         for h in group:
-            for kv in range(2):
-                @pl.when(pos > 0)
-                def _():
-                    halo(0, kv, h).wait_recv()
-
-                @pl.when(pos < last)
-                def _():
-                    halo(1, kv, h).wait_recv()
+            each_arrival(halo, h)
         for p in range(pairs):
             r = pl.ds(p * PAIR, PAIR)
             w = pl.ds(p * PAIR, WINDOW)
             squares, products = sq[r, :], inner[r, :]
             for h in group:
                 c = cols(h)
-                scores = dot(kext[w, c], q[r, c], NT) * scale
+                scores = dot(kvext[h, 0, w], q[r, c], NT) * scale
                 total = None
                 for strand, kept in ((0, w1s), (1, w2s)):
                     s = scores + bias[strand, p]
@@ -172,7 +176,7 @@
                     e = e * (1.0 / jnp.sum(e, axis=0, keepdims=True))
                     kept[h, p] = e
                     total = e if total is None else total + e
-                m = dot(total.astype(jnp.bfloat16), vext[w, c], TN)
+                m = dot(total.astype(jnp.bfloat16), kvext[h, 1, w], TN)
                 mixed[r, c] = m
                 squares = squares + m * m
                 products = products + gain_ref[pl.ds(h, 1), :] * og[r, c].astype(jnp.float32) * m
@@ -234,12 +238,12 @@
     out_copies = [pltpu.make_async_copy(normed, normed_hbm, store_sem.at[0])]
     out_copies[0].start()
 
-    def back(way, kv, h):
+    def back(way, h):
         return pltpu.make_async_remote_copy(
-            src_ref=out_halo.at[way, kv, :, cols(h)],
-            dst_ref=in_halo.at[way, kv, :, cols(h)],
-            send_sem=bsend.at[way, kv, h],
-            recv_sem=brecv.at[way, kv, h],
+            src_ref=out_halo.at[way, h],
+            dst_ref=in_halo.at[way, h],
+            send_sem=bsend.at[way, h],
+            recv_sem=brecv.at[way, h],
             device_id=((right, left)[way], me_h),
             device_id_type=MESH,
         )
@@ -254,17 +258,17 @@
                 w = pl.ds(p * PAIR, WINDOW)
                 g = grad[r, c]
                 w1, w2 = w1s[h, p], w2s[h, p]
-                wg = dot(vext[w, c], g, NT)
+                wg = dot(kvext[h, 1, w], g, NT)
                 c1 = jnp.sum(w1 * wg, axis=0, keepdims=True)
                 c2 = jnp.sum(w2 * wg, axis=0, keepdims=True)
                 ds = ((w1 * (wg - c1) + w2 * (wg - c2)) * scale).astype(jnp.bfloat16)
                 dvw = dot((w1 + w2).astype(jnp.bfloat16), g, NN)
                 dkw = dot(ds, q[r, c], NN)
-                dq[r, c] = dot(ds, kext[w, c], TN).astype(jnp.bfloat16)
+                dq[r, c] = dot(ds, kvext[h, 0, w], TN).astype(jnp.bfloat16)
                 parts.append((dkw, dvw))
             for kv, own in ((0, dk), (1, dv)):
-                out_halo[1, kv, :, c] = parts[0][kv][0:RIM].astype(jnp.bfloat16)
-                out_halo[0, kv, :, c] = parts[-1][kv][WINDOW - RIM :].astype(jnp.bfloat16)
+                out_halo[1, h, kv] = parts[0][kv][0:RIM].astype(jnp.bfloat16)
+                out_halo[0, h, kv] = parts[-1][kv][WINDOW - RIM :].astype(jnp.bfloat16)
                 for p in range(pairs):
                     mid = parts[p][kv][RIM : RIM + PAIR]
                     if p > 0:
@@ -273,14 +277,7 @@
                         mid = mid + parts[p + 1][kv][0:RIM]
                     own[pl.ds(p * PAIR, PAIR), c] = mid
         for h in group:
-            for kv in range(2):
-                @pl.when(pos < last)
-                def _():
-                    back(0, kv, h).start()
-
-                @pl.when(pos > 0)
-                def _():
-                    back(1, kv, h).start()
+            each_way(lambda copy: copy.start(), back, h)
         return carry
 
     lax.fori_loop(0, heads // GROUP, backward, 0)
@@ -305,17 +302,11 @@
 
     def settle(h, carry):
         c = cols(h)
+        each_arrival(back, h)
         for kv, own, out in ((0, dk, dko), (1, dv, dvo)):
-            @pl.when(pos > 0)
-            def _():
-                back(0, kv, h).wait_recv()
-
-            @pl.when(pos < last)
-            def _():
-                back(1, kv, h).wait_recv()
-            out[0:RIM, c] = (own[0:RIM, c] + in_halo[0, kv, :, c].astype(jnp.float32)).astype(jnp.bfloat16)
+            out[0:RIM, c] = (own[0:RIM, c] + in_halo[0, h, kv].astype(jnp.float32)).astype(jnp.bfloat16)
             out[rows - RIM : rows, c] = (
-                own[rows - RIM : rows, c] + in_halo[1, kv, :, c].astype(jnp.float32)
+                own[rows - RIM : rows, c] + in_halo[1, h, kv].astype(jnp.float32)
             ).astype(jnp.bfloat16)
         return carry
 
@@ -331,20 +322,9 @@
     for o in range(1, n_ctx):
         share(pos, o, lax.rem(pos + o, n_ctx)).wait_send()
 
-    def drain(h, carry):
-        for kv in range(2):
-            @pl.when(pos < last)
-            def _():
-                halo(0, kv, h).wait_send()
-                back(0, kv, h).wait_send()
-
-            @pl.when(pos > 0)
-            def _():
-                halo(1, kv, h).wait_send()
-                back(1, kv, h).wait_send()
-        return carry
-
-    lax.fori_loop(0, heads, drain, 0)
+    for h in range(heads):
+        each_way(lambda copy: copy.wait_send(), halo, h)
+        each_way(lambda copy: copy.wait_send(), back, h)
     for copy in out_copies:
         copy.wait()
 
@@ -386,8 +366,7 @@
             pltpu.VMEM(block_mask.shape, jnp.int32),
             pltpu.VMEM(norm_gain.shape, f32),
             pltpu.VMEM((rows, features), bf),
-            pltpu.VMEM((ext, features), bf),
-            pltpu.VMEM((ext, features), bf),
+            pltpu.VMEM((heads, 2, ext, D), bf),
             pltpu.VMEM((rows, features), bf),
             pltpu.VMEM((8, 128), jnp.int32),
             pltpu.VMEM((8, 128), jnp.int32),
@@ -408,20 +387,21 @@
             pltpu.VMEM((rows, features), f32),
             pltpu.VMEM((rows, features), bf),
             pltpu.VMEM((rows, features), bf),
-            pltpu.VMEM((2, 2, RIM, features), bf),
-            pltpu.VMEM((2, 2, RIM, features), bf),
-            dma((6,)),
-            dma((2, 2, heads)),
-            dma((2, 2, heads)),
+            pltpu.VMEM((2, heads, 2, RIM, D), bf),
+            pltpu.VMEM((2, heads, 2, RIM, D), bf),
+            dma((4,)),
+            dma((2, heads)),
+            dma((2, heads)),
             dma,
             dma,
             dma((n_head,)),
             dma((n_head,)),
             dma((n_ctx,)),
             dma((n_ctx,)),
-            dma((2, 2, heads)),
-            dma((2, 2, heads)),
+            dma((2, heads)),
+            dma((2, heads)),
             dma((4,)),
+            dma((2, heads)),
         ],
         compiler_params=pltpu.CompilerParams(
             collective_id=0, has_side_effects=True, vmem_limit_bytes=VMEM

time: 39.1 us -> 38.4 us (0.982)
  Pallas kernels: 38.3 us -> 37.6 us
    pallas_call x1, Pallas kernels: 35.9 us -> 35.2 us  [body(): pl.pallas_call(functools.partial(kernel, n_ctx, n_head), out_shape=(big,...]
where the time goes in v5:
time: 38.4 us; the launch traced here: 38.3 us
  Pallas kernels  37.6 us (98%)
  between operations  0.64 us (2%)
    pallas_call x1, Pallas kernels, body(): pl.pallas_call(functools.partial(kernel, n_ctx, n_head), out_shape=(big,...  35.2 us
    pallas_call x1, Pallas kernels, body(): pl.pallas_call(store_kernel, out_shape=tuple((jax.ShapeDtypeStruct(x.shap...  2.44 us

profile of v5, /device:TPU:4, one launch (start us, length us, event | category | flops | bytes accessed | tf_op | source)
XLA Modules:
  0.0 38.3 jit_solution(10045030610002994571)
XLA Ops:
  0.6 35.2 %strand_attention.1 = (bf16[256,1024]{1,0:T(8,128)(2,1)}, bf16[256,1024]{1,0:T(8,128)(2,1)}, bf16[256,1024]{1,0:T(8,128)(2,1)}, bf16[256,1024]{1,0:T(8,128)(2,1)}, f32[8,128]{1,0:T(8,128)}) custom-call(bf16[256,1024]{1,0:T(8,128)(2,1)} %q_hbm.1, bf16[256,1024]{1,0:T(8,128)(2,1)} %k_hbm.1, bf16[256,1024]{1,0:T(8,128)(2,1)} %v_hbm.1, ...), custom_call_target="tpu_custom_call" | custom-call | tf_op jit(solution)/shard_map/strand_attention/pallas_call | solution.py:360
  35.8 2.4 %store_results.1 = (bf16[256,1024]{1,0:T(8,128)(2,1)}, bf16[256,1024]{1,0:T(8,128)(2,1)}, bf16[256,1024]{1,0:T(8,128)(2,1)}, bf16[256,1024]{1,0:T(8,128)(2,1)}, f32[8,128]{1,0:T(8,128)}) custom-call(bf16[256,1024]{1,0:T(8,128)(2,1)} %get-tuple-element.10.refs_0_, bf16[256,1024]{1,0:T(8,128)(2,1)} %get-tuple-element.11.refs_1_, ...), custom_call_target="tpu_custom_call" | custom-call | tf_op jit(solution)/shard_map/store_results/pallas_call | solution.py:411

commit v6 on v5

--- a/solution.py
+++ b/solution.py
@@ -32,7 +32,7 @@
     normed_hbm, dq_hbm, dk_hbm, dv_hbm, gg_ref,
     mask_ref, gain_ref, q, kvext, og, mine, theirs, bias, w1s, w2s, mixed, sq, inner, sall, invs, coefs,
     grad, gall, normed, dq, dk, dv, dko, dvo, out_halo, in_halo,
-    load_sem, fsend, frecv, msend, mrecv, ssend, srecv, gsend, grecv, bsend, brecv, store_sem, kv_sem,
+    load_sem, fsend, frecv, msend, mrecv, ssend, srecv, gsend, grecv, bsend, brecv, store_sem, kv_sem, relay, asend, rsend, rrecv,
 ):
     pos = lax.axis_index("ctx")
     me_h = lax.axis_index("head")
@@ -110,14 +110,54 @@
     for copy in kv_loads:
         copy.wait()
 
-    def each_way(act, plain, h):
-        @pl.when(pos < last)
-        def _():
-            act(plain(0, h))
-
-        @pl.when(pos > 0)
-        def _():
-            act(plain(1, h))
+    square = n_ctx == 8
+    ends = (n_ctx // 2 - 1, n_ctx // 2)
+    corners = (0, last)
+
+    def first_leg(way, phase, step):
+        h = step * GROUP + 1
+        src = kvext.at[h, :, pl.ds((rows, RIM)[way], RIM)] if phase == 0 else out_halo.at[way, h]
+        return pltpu.make_async_remote_copy(
+            src_ref=src, dst_ref=relay.at[phase, step],
+            send_sem=asend.at[phase, step], recv_sem=rrecv.at[phase, step],
+            device_id=(corners[way], me_h), device_id_type=MESH,
+        )
+
+    def second_leg(way, phase, step):
+        h = step * GROUP + 1
+        if phase == 0:
+            dst, sem = kvext.at[h, :, pl.ds((0, rows + RIM)[way], RIM)], frecv.at[way, h]
+        else:
+            dst, sem = in_halo.at[way, h], brecv.at[way, h]
+        return pltpu.make_async_remote_copy(
+            src_ref=relay.at[phase, step], dst_ref=dst,
+            send_sem=rsend.at[phase, step], recv_sem=sem,
+            device_id=(ends[1 - way], me_h), device_id_type=MESH,
+        )
+
+    def pass_on(phase, step):
+        if square:
+            for way in range(2):
+                @pl.when(pos == corners[way])
+                def _():
+                    first_leg(way, phase, step).wait_recv()
+                    second_leg(way, phase, step).start()
+
+    def each_send(phase, step, plain, act):
+        for i in range(GROUP):
+            h = step * GROUP + i
+            for way in range(2):
+                able = (pos < last, pos > 0)[way]
+                if square and i == 1:
+                    @pl.when(pos == ends[way])
+                    def _():
+                        act(first_leg(way, phase, step))
+
+                    able = able & (pos != ends[way])
+
+                @pl.when(able)
+                def _():
+                    act(plain(way, h))
 
     def each_arrival(plain, h):
         @pl.when(pos > 0)
@@ -128,8 +168,8 @@
         def _():
             plain(1, h).wait_recv()
 
-    for h in range(heads):
-        each_way(lambda copy: copy.start(), halo, h)
+    for step in range(heads // GROUP):
+        each_send(0, step, halo, lambda copy: copy.start())
     mirror.wait_recv()
 
     all_blocks = blocks_dev * n_ctx
@@ -160,6 +200,7 @@
 
     def forward(step, carry):
         group = [step * GROUP + i for i in range(GROUP)]
+        pass_on(0, step)
         for h in group:
             each_arrival(halo, h)
         for p in range(pairs):
@@ -276,11 +317,16 @@
                     if p < pairs - 1:
                         mid = mid + parts[p + 1][kv][0:RIM]
                     own[pl.ds(p * PAIR, PAIR), c] = mid
-        for h in group:
-            each_way(lambda copy: copy.start(), back, h)
+        each_send(1, step, back, lambda copy: copy.start())
+
+        @pl.when(step > 0)
+        def _():
+            pass_on(1, step - 1)
+
         return carry
 
     lax.fori_loop(0, heads // GROUP, backward, 0)
+    pass_on(1, heads // GROUP - 1)
     dq_copy = pltpu.make_async_copy(dq, dq_hbm, store_sem.at[1])
     dq_copy.start()
     out_copies.append(dq_copy)
@@ -322,9 +368,14 @@
     for o in range(1, n_ctx):
         share(pos, o, lax.rem(pos + o, n_ctx)).wait_send()
 
-    for h in range(heads):
-        each_way(lambda copy: copy.wait_send(), halo, h)
-        each_way(lambda copy: copy.wait_send(), back, h)
+    for step in range(heads // GROUP):
+        for phase, plain in ((0, halo), (1, back)):
+            each_send(phase, step, plain, lambda copy: copy.wait_send())
+            if square:
+                for way in range(2):
+                    @pl.when(pos == corners[way])
+                    def _():
+                        second_leg(way, phase, step).wait_send()
     for copy in out_copies:
         copy.wait()
 
@@ -402,6 +453,10 @@
             dma((2, heads)),
             dma((4,)),
             dma((2, heads)),
+            pltpu.VMEM((2, heads // GROUP, 2, RIM, D), bf),
+            dma((2, heads // GROUP)),
+            dma((2, heads // GROUP)),
+            dma((2, heads // GROUP)),
         ],
         compiler_params=pltpu.CompilerParams(
             collective_id=0, has_side_effects=True, vmem_limit_bytes=VMEM

time: 38.4 us -> 42.9 us (1.12)
  the two profiles are of different devices: /device:TPU:4 before, /device:TPU:3 now
where the time goes in v6:
time: 42.9 us; the launch traced here: 42.8 us
  Pallas kernels  42.1 us (98%)
  between operations  0.64 us (1%)
    pallas_call x1, Pallas kernels, body(): pl.pallas_call(functools.partial(kernel, n_ctx, n_head), out_shape=(big,...  39.7 us
    pallas_call x1, Pallas kernels, body(): pl.pallas_call(store_kernel, out_shape=tuple((jax.ShapeDtypeStruct(x.shap...  2.44 us

profile of v6, /device:TPU:3, one launch (start us, length us, event | category | flops | bytes accessed | tf_op | source)
XLA Modules:
  0.0 42.8 jit_solution(5090855119341072278)
XLA Ops:
  0.6 39.7 %strand_attention.1 = (bf16[256,1024]{1,0:T(8,128)(2,1)}, bf16[256,1024]{1,0:T(8,128)(2,1)}, bf16[256,1024]{1,0:T(8,128)(2,1)}, bf16[256,1024]{1,0:T(8,128)(2,1)}, f32[8,128]{1,0:T(8,128)}) custom-call(bf16[256,1024]{1,0:T(8,128)(2,1)} %q_hbm.1, bf16[256,1024]{1,0:T(8,128)(2,1)} %k_hbm.1, bf16[256,1024]{1,0:T(8,128)(2,1)} %v_hbm.1, ...), custom_call_target="tpu_custom_call" | custom-call | tf_op jit(solution)/shard_map/strand_attention/pallas_call | solution.py:411
  40.3 2.4 %store_results.1 = (bf16[256,1024]{1,0:T(8,128)(2,1)}, bf16[256,1024]{1,0:T(8,128)(2,1)}, bf16[256,1024]{1,0:T(8,128)(2,1)}, bf16[256,1024]{1,0:T(8,128)(2,1)}, f32[8,128]{1,0:T(8,128)}) custom-call(bf16[256,1024]{1,0:T(8,128)(2,1)} %get-tuple-element.10.refs_0_, bf16[256,1024]{1,0:T(8,128)(2,1)} %get-tuple-element.11.refs_1_, ...), custom_call_target="tpu_custom_call" | custom-call | tf_op jit(solution)/shard_map/store_results/pallas_call | solution.py:466

commit v7 on v5

--- a/solution.py
+++ b/solution.py
@@ -32,7 +32,7 @@
     normed_hbm, dq_hbm, dk_hbm, dv_hbm, gg_ref,
     mask_ref, gain_ref, q, kvext, og, mine, theirs, bias, w1s, w2s, mixed, sq, inner, sall, invs, coefs,
     grad, gall, normed, dq, dk, dv, dko, dvo, out_halo, in_halo,
-    load_sem, fsend, frecv, msend, mrecv, ssend, srecv, gsend, grecv, bsend, brecv, store_sem, kv_sem,
+    load_sem, fsend, frecv, msend, mrecv, ssend, srecv, gsend, grecv, bsend, brecv, store_sem, kv_sem, relay, asend, rsend, rrecv,
 ):
     pos = lax.axis_index("ctx")
     me_h = lax.axis_index("head")
@@ -110,14 +110,57 @@
     for copy in kv_loads:
         copy.wait()
 
-    def each_way(act, plain, h):
-        @pl.when(pos < last)
-        def _():
-            act(plain(0, h))
-
-        @pl.when(pos > 0)
-        def _():
-            act(plain(1, h))
+    square = n_ctx == 8
+    ends = (n_ctx // 2 - 1, n_ctx // 2)
+    corners = (last, 0)
+    half = heads // 2
+
+    def first_leg(way, phase, j):
+        h = half + j if phase == 0 else j
+        src = kvext.at[h, :, pl.ds((rows, RIM)[way], RIM)] if phase == 0 else out_halo.at[way, h]
+        return pltpu.make_async_remote_copy(
+            src_ref=src, dst_ref=relay.at[phase, j],
+            send_sem=asend.at[phase, j], recv_sem=rrecv.at[phase, j],
+            device_id=(corners[way], me_h), device_id_type=MESH,
+        )
+
+    def second_leg(way, phase, j):
+        h = half + j if phase == 0 else j
+        if phase == 0:
+            dst, sem = kvext.at[h, :, pl.ds((0, rows + RIM)[way], RIM)], frecv.at[way, h]
+        else:
+            dst, sem = in_halo.at[way, h], brecv.at[way, h]
+        return pltpu.make_async_remote_copy(
+            src_ref=relay.at[phase, j], dst_ref=dst,
+            send_sem=rsend.at[phase, j], recv_sem=sem,
+            device_id=(ends[1 - way], me_h), device_id_type=MESH,
+        )
+
+    def pass_on(phase, j):
+        if square:
+            for way in range(2):
+                @pl.when(pos == corners[way])
+                def _():
+                    first_leg(way, phase, j).wait_recv()
+                    second_leg(way, phase, j).start()
+
+    def each_detour(phase, j, act):
+        if square:
+            for way in range(2):
+                @pl.when(pos == ends[way])
+                def _():
+                    act(first_leg(way, phase, j))
+
+    def each_direct(phase, h, plain, act):
+        detoured = (h >= half) if phase == 0 else (h < half)
+        for way in range(2):
+            able = (pos < last, pos > 0)[way]
+            if square:
+                able = able & jnp.logical_not((pos == ends[way]) & detoured)
+
+            @pl.when(able)
+            def _():
+                act(plain(way, h))
 
     def each_arrival(plain, h):
         @pl.when(pos > 0)
@@ -129,7 +172,9 @@
             plain(1, h).wait_recv()
 
     for h in range(heads):
-        each_way(lambda copy: copy.start(), halo, h)
+        if h < half:
+            each_detour(0, h, lambda copy: copy.start())
+        each_direct(0, h, halo, lambda copy: copy.start())
     mirror.wait_recv()
 
     all_blocks = blocks_dev * n_ctx
@@ -160,6 +205,13 @@
 
     def forward(step, carry):
         group = [step * GROUP + i for i in range(GROUP)]
+        for i in range(GROUP):
+            j = step * GROUP + i
+
+            @pl.when(j < half)
+            def _():
+                pass_on(0, j)
+
         for h in group:
             each_arrival(halo, h)
         for p in range(pairs):
@@ -277,7 +329,17 @@
                         mid = mid + parts[p + 1][kv][0:RIM]
                     own[pl.ds(p * PAIR, PAIR), c] = mid
         for h in group:
-            each_way(lambda copy: copy.start(), back, h)
+            @pl.when(h < half)
+            def _():
+                each_detour(1, h, lambda copy: copy.start())
+
+            each_direct(1, h, back, lambda copy: copy.start())
+
+        for h in group:
+            @pl.when((h >= GROUP) & (h < half + GROUP))
+            def _():
+                pass_on(1, h - GROUP)
+
         return carry
 
     lax.fori_loop(0, heads // GROUP, backward, 0)
@@ -322,9 +384,16 @@
     for o in range(1, n_ctx):
         share(pos, o, lax.rem(pos + o, n_ctx)).wait_send()
 
-    for h in range(heads):
-        each_way(lambda copy: copy.wait_send(), halo, h)
-        each_way(lambda copy: copy.wait_send(), back, h)
+    for phase, plain in ((0, halo), (1, back)):
+        for h in range(heads):
+            each_direct(phase, h, plain, lambda copy: copy.wait_send())
+        for j in range(half):
+            each_detour(phase, j, lambda copy: copy.wait_send())
+            if square:
+                for way in range(2):
+                    @pl.when(pos == corners[way])
+                    def _():
+                        second_leg(way, phase, j).wait_send()
     for copy in out_copies:
         copy.wait()
 
@@ -402,6 +471,10 @@
             dma((2, heads)),
             dma((4,)),
             dma((2, heads)),
+            pltpu.VMEM((2, heads // 2, 2, RIM, D), bf),
+            dma((2, heads // 2)),
+            dma((2, heads // 2)),
+            dma((2, heads // 2)),
         ],
         compiler_params=pltpu.CompilerParams(
             collective_id=0, has_side_effects=True, vmem_limit_bytes=VMEM

time: 38.4 us -> 38.8 us (1.010)
  the two profiles are of different devices: /device:TPU:4 before, /device:TPU:1 now
where the time goes in v7:
time: 38.8 us; the launch traced here: 38.6 us
  Pallas kernels  38 us (98%)
  between operations  0.64 us (2%)
    pallas_call x1, Pallas kernels, body(): pl.pallas_call(functools.partial(kernel, n_ctx, n_head), out_shape=(big,...  35.6 us
    pallas_call x1, Pallas kernels, body(): pl.pallas_call(store_kernel, out_shape=tuple((jax.ShapeDtypeStruct(x.shap...  2.44 us

profile of v7, /device:TPU:1, one launch (start us, length us, event | category | flops | bytes accessed | tf_op | source)
XLA Modules:
  0.0 38.6 jit_solution(14089199692651213423)
XLA Ops:
  0.6 35.6 %strand_attention.1 = (bf16[256,1024]{1,0:T(8,128)(2,1)}, bf16[256,1024]{1,0:T(8,128)(2,1)}, bf16[256,1024]{1,0:T(8,128)(2,1)}, bf16[256,1024]{1,0:T(8,128)(2,1)}, f32[8,128]{1,0:T(8,128)}) custom-call(bf16[256,1024]{1,0:T(8,128)(2,1)} %q_hbm.1, bf16[256,1024]{1,0:T(8,128)(2,1)} %k_hbm.1, bf16[256,1024]{1,0:T(8,128)(2,1)} %v_hbm.1, ...), custom_call_target="tpu_custom_call" | custom-call | tf_op jit(solution)/shard_map/strand_attention/pallas_call | solution.py:429
  36.2 2.4 %store_results.1 = (bf16[256,1024]{1,0:T(8,128)(2,1)}, bf16[256,1024]{1,0:T(8,128)(2,1)}, bf16[256,1024]{1,0:T(8,128)(2,1)}, bf16[256,1024]{1,0:T(8,128)(2,1)}, f32[8,128]{1,0:T(8,128)}) custom-call(bf16[256,1024]{1,0:T(8,128)(2,1)} %get-tuple-element.10.refs_0_, bf16[256,1024]{1,0:T(8,128)(2,1)} %get-tuple-element.11.refs_1_, ...), custom_call_target="tpu_custom_call" | custom-call | tf_op jit(solution)/shard_map/store_results/pallas_call | solution.py:484

commit v8 on v5

--- a/solution.py
+++ b/solution.py
@@ -15,7 +15,7 @@
 PAIR = 2 * BLOCK
 WINDOW = PAIR + 2 * RIM
 VMEM = 64 * 1024 * 1024
-GROUP = 2
+GROUP = 1
 MESH = pl.DeviceIdType.MESH
 NT = (((1,), (1,)), ((), ()))
 TN = (((0,), (0,)), ((), ()))
@@ -30,9 +30,9 @@
     n_ctx, n_head,
     q_hbm, k_hbm, v_hbm, og_hbm, mask_hbm, gain_hbm,
     normed_hbm, dq_hbm, dk_hbm, dv_hbm, gg_ref,
-    mask_ref, gain_ref, q, kvext, og, mine, theirs, bias, w1s, w2s, mixed, sq, inner, sall, invs, coefs,
+    mask_ref, gain_ref, q, kvext, og, mine, theirs, bias, w1s, w2s, wsum, mixed, sq, inner, sall, invs, coefs,
     grad, gall, normed, dq, dk, dv, dko, dvo, out_halo, in_halo,
-    load_sem, fsend, frecv, msend, mrecv, ssend, srecv, gsend, grecv, bsend, brecv, store_sem, kv_sem,
+    load_sem, fsend, frecv, msend, mrecv, ssend, srecv, gsend, grecv, bsend, brecv, store_sem, kv_sem, out_sem,
 ):
     pos = lax.axis_index("ctx")
     me_h = lax.axis_index("head")
@@ -176,7 +176,9 @@
                     e = e * (1.0 / jnp.sum(e, axis=0, keepdims=True))
                     kept[h, p] = e
                     total = e if total is None else total + e
-                m = dot(total.astype(jnp.bfloat16), kvext[h, 1, w], TN)
+                both = total.astype(jnp.bfloat16)
+                wsum[h, p] = both
+                m = dot(both, kvext[h, 1, w], TN)
                 mixed[r, c] = m
                 squares = squares + m * m
                 products = products + gain_ref[pl.ds(h, 1), :] * og[r, c].astype(jnp.float32) * m
@@ -262,7 +264,7 @@
                 c1 = jnp.sum(w1 * wg, axis=0, keepdims=True)
                 c2 = jnp.sum(w2 * wg, axis=0, keepdims=True)
                 ds = ((w1 * (wg - c1) + w2 * (wg - c2)) * scale).astype(jnp.bfloat16)
-                dvw = dot((w1 + w2).astype(jnp.bfloat16), g, NN)
+                dvw = dot(wsum[h, p], g, NN)
                 dkw = dot(ds, q[r, c], NN)
                 dq[r, c] = dot(ds, kvext[h, 0, w], TN).astype(jnp.bfloat16)
                 parts.append((dkw, dvw))
@@ -300,6 +302,11 @@
     def _():
         in_halo[1] = jnp.zeros(in_halo.shape[1:], in_halo.dtype)
 
+    def result(i, h):
+        return pltpu.make_async_copy(
+            (dko, dvo)[i].at[:, cols(h)], (dk_hbm, dv_hbm)[i].at[:, cols(h)], out_sem.at[i, h]
+        )
+
     def settle(h, carry):
         c = cols(h)
         each_arrival(back, h)
@@ -308,13 +315,13 @@
             out[rows - RIM : rows, c] = (
                 own[rows - RIM : rows, c] + in_halo[1, h, kv].astype(jnp.float32)
             ).astype(jnp.bfloat16)
+        for i in range(2):
+            result(i, h).start()
         return carry
 
     lax.fori_loop(0, heads, settle, 0)
-    for i, (src, dst) in enumerate(((dko, dk_hbm), (dvo, dv_hbm))):
-        copy = pltpu.make_async_copy(src, dst, store_sem.at[2 + i])
-        copy.start()
-        out_copies.append(copy)
+    for h in range(heads):
+        out_copies.extend(result(i, h) for i in range(2))
 
     mirror.wait_send()
     for o in range(1, n_head):
@@ -373,6 +380,7 @@
             pltpu.VMEM((2, pairs, WINDOW, PAIR), f32),
             pltpu.VMEM((heads, pairs, WINDOW, PAIR), f32),
             pltpu.VMEM((heads, pairs, WINDOW, PAIR), f32),
+            pltpu.VMEM((heads, pairs, WINDOW, PAIR), bf),
             pltpu.VMEM((rows, features), f32),
             pltpu.VMEM((rows, D), f32),
             pltpu.VMEM((rows, D), f32),
@@ -401,6 +409,7 @@
             dma((2, heads)),
             dma((2, heads)),
             dma((4,)),
+            dma((2, heads)),
             dma((2, heads)),
         ],
         compiler_params=pltpu.CompilerParams(

time: 38.4 us -> 37.6 us (0.979)
  Pallas kernels: 37.6 us -> 36.8 us
    pallas_call x1, Pallas kernels: 35.2 us -> 34.3 us  [body(): pl.pallas_call(functools.partial(kernel, n_ctx, n_head), out_shape=(big,...]
where the time goes in v8:
time: 37.6 us; the launch traced here: 37.4 us
  Pallas kernels  36.8 us (98%)
  between operations  0.64 us (2%)
    pallas_call x1, Pallas kernels, body(): pl.pallas_call(functools.partial(kernel, n_ctx, n_head), out_shape=(big,...  34.3 us
    pallas_call x1, Pallas kernels, body(): pl.pallas_call(store_kernel, out_shape=tuple((jax.ShapeDtypeStruct(x.shap...  2.44 us

profile of v8, /device:TPU:4, one launch (start us, length us, event | category | flops | bytes accessed | tf_op | source)
XLA Modules:
  0.0 37.4 jit_solution(2733954453327648871)
XLA Ops:
  0.6 34.3 %strand_attention.1 = (bf16[256,1024]{1,0:T(8,128)(2,1)}, bf16[256,1024]{1,0:T(8,128)(2,1)}, bf16[256,1024]{1,0:T(8,128)(2,1)}, bf16[256,1024]{1,0:T(8,128)(2,1)}, f32[8,128]{1,0:T(8,128)}) custom-call(bf16[256,1024]{1,0:T(8,128)(2,1)} %q_hbm.1, bf16[256,1024]{1,0:T(8,128)(2,1)} %k_hbm.1, bf16[256,1024]{1,0:T(8,128)(2,1)} %v_hbm.1, ...), custom_call_target="tpu_custom_call" | custom-call | tf_op jit(solution)/shard_map/strand_attention/pallas_call | solution.py:367
  35.0 2.4 %store_results.1 = (bf16[256,1024]{1,0:T(8,128)(2,1)}, bf16[256,1024]{1,0:T(8,128)(2,1)}, bf16[256,1024]{1,0:T(8,128)(2,1)}, bf16[256,1024]{1,0:T(8,128)(2,1)}, f32[8,128]{1,0:T(8,128)}) custom-call(bf16[256,1024]{1,0:T(8,128)(2,1)} %get-tuple-element.10.refs_0_, bf16[256,1024]{1,0:T(8,128)(2,1)} %get-tuple-element.11.refs_1_, ...), custom_call_target="tpu_custom_call" | custom-call | tf_op jit(solution)/shard_map/store_results/pallas_call | solution.py:420

commit v9 on v8

--- a/solution.py
+++ b/solution.py
@@ -107,8 +107,6 @@
     )
     mirror.start()
 
-    for copy in kv_loads:
-        copy.wait()
 
     def each_way(act, plain, h):
         @pl.when(pos < last)
@@ -129,6 +127,8 @@
             plain(1, h).wait_recv()
 
     for h in range(heads):
+        kv_loads[2 * h].wait()
+        kv_loads[2 * h + 1].wait()
         each_way(lambda copy: copy.start(), halo, h)
     mirror.wait_recv()
 

time: 37.6 us -> 37.6 us (level)
  no operation moved by 1% of the time
where the time goes in v9:
time: 37.6 us; the launch traced here: 37.4 us
  Pallas kernels  36.8 us (98%)
  between operations  0.64 us (2%)
    pallas_call x1, Pallas kernels, body(): pl.pallas_call(functools.partial(kernel, n_ctx, n_head), out_shape=(big,...  34.3 us
    pallas_call x1, Pallas kernels, body(): pl.pallas_call(store_kernel, out_shape=tuple((jax.ShapeDtypeStruct(x.shap...  2.44 us

profile of v9, /device:TPU:4, one launch (start us, length us, event | category | flops | bytes accessed | tf_op | source)
XLA Modules:
  0.0 37.4 jit_solution(17034257408276923121)
XLA Ops:
  0.6 34.3 %strand_attention.1 = (bf16[256,1024]{1,0:T(8,128)(2,1)}, bf16[256,1024]{1,0:T(8,128)(2,1)}, bf16[256,1024]{1,0:T(8,128)(2,1)}, bf16[256,1024]{1,0:T(8,128)(2,1)}, f32[8,128]{1,0:T(8,128)}) custom-call(bf16[256,1024]{1,0:T(8,128)(2,1)} %q_hbm.1, bf16[256,1024]{1,0:T(8,128)(2,1)} %k_hbm.1, bf16[256,1024]{1,0:T(8,128)(2,1)} %v_hbm.1, ...), custom_call_target="tpu_custom_call" | custom-call | tf_op jit(solution)/shard_map/strand_attention/pallas_call | solution.py:367
  35.0 2.4 %store_results.1 = (bf16[256,1024]{1,0:T(8,128)(2,1)}, bf16[256,1024]{1,0:T(8,128)(2,1)}, bf16[256,1024]{1,0:T(8,128)(2,1)}, bf16[256,1024]{1,0:T(8,128)(2,1)}, f32[8,128]{1,0:T(8,128)}) custom-call(bf16[256,1024]{1,0:T(8,128)(2,1)} %get-tuple-element.10.refs_0_, bf16[256,1024]{1,0:T(8,128)(2,1)} %get-tuple-element.11.refs_1_, ...), custom_call_target="tpu_custom_call" | custom-call | tf_op jit(solution)/shard_map/store_results/pallas_call | solution.py:420
